TPU v7x, 32 devices: a whole 2x2x4 slice. The times are simulated.
32 devices in a mesh: dp: 8 (over z, x), tensor: 4 (over y, core).
Axes of the slice: x: 2, y: 2, z: 4, core: 2. Of those that a mesh axis runs over, the one named last changes fastest.
Arguments:
- tokens: bfloat16 [16384, 1024], P(('dp', 'tensor')), may hold values from -6 to 6
- segments: int32 [16384], P('dp'), may hold values from 0 to 4, as said below
- norm_gains: bfloat16 [2, 1024], P(None, 'dp'), may hold values from 0.099609375 to 1.8984375
- norm_biases: bfloat16 [2, 1024], P(None, 'dp'), may hold values from -3 to 3
- qkv_weight: bfloat16 [1024, 3, 1024], P('dp', None, 'tensor'), may hold values from -0.1875 to 0.1875
- qv_bias: bfloat16 [16, 128], P('tensor', 'dp'), may hold values from -4 to 4
- out_weight: bfloat16 [1024, 1024], P('tensor', 'dp'), may hold values from -0.75 to 0.75
- out_bias: bfloat16 [1024], P('dp'), may hold values from -4 to 4
- up_weight: bfloat16 [1024, 4096], P('dp', 'tensor'), may hold values from -0.1875 to 0.1875
- up_bias: bfloat16 [32, 128], P('tensor', 'dp'), may hold values from -4 to 4
- down_weight: bfloat16 [4096, 1024], P('tensor', 'dp'), may hold values from -0.09375 to 0.09375
- down_bias: bfloat16 [1024], P('dp'), may hold values from -4 to 4
- out_grad: bfloat16 [16384, 1024], P(('dp', 'tensor')), may hold values from -6 to 6
Outputs:
- output: bfloat16 [16384, 1024], P(('dp', 'tensor'))
- input_grad: float32 [16384, 1024], P(('dp', 'tensor'))
- norm_gains_grad: float32 [2, 1024], P(None, 'dp')
- norm_biases_grad: float32 [2, 1024], P(None, 'dp')
- qkv_weight_grad: float32 [1024, 3, 1024], P('dp', None, 'tensor')
- qv_bias_grad: float32 [16, 128], P('tensor', 'dp')
- out_weight_grad: float32 [1024, 1024], P('tensor', 'dp')
- out_bias_grad: float32 [1024], P('dp')
- up_weight_grad: float32 [1024, 4096], P('dp', 'tensor')
- up_bias_grad: float32 [32, 128], P('tensor', 'dp')
- down_weight_grad: float32 [4096, 1024], P('tensor', 'dp')
- down_bias_grad: float32 [1024], P('dp')
Inputs may be any that keep to these rules, and one draw needn't show every extreme that they name: `segments`: within each packed sequence of 2048 tokens the document numbers never fall; every sequence holds five documents, numbered from 0.
All inputs are finite; a program needn't handle non-finite values.
Results may differ from a plain program's by a relative error of at most 0.017.
Values may be sent and summed in bfloat16 or wider, within the bound.
A program may use at most 192 MiB of HBM per device.

v0:
```python
from functools import partial

import jax
import jax.numpy as jnp
from jax import lax
from jax.sharding import PartitionSpec as P

D = 1024
H = 16
HD = 64


EPS = 1e-05


def norm_rows(values, gain, shift):
    centre = jnp.mean(values, axis=-1, keepdims=True)
    centred = values - centre
    spread = jnp.mean(centred * centred, axis=-1, keepdims=True)
    return centred * lax.rsqrt(spread + EPS) * gain + shift


def head_slopes(local_heads):
    index = lax.axis_index("tensor") * local_heads + jnp.arange(local_heads)
    return 2.0 ** (-8.0 * (index.astype(jnp.float32) + 1.0) / H)


def gather_rows(values):
    return lax.all_gather(values, "tensor", axis=0, tiled=True)


def spread_rows(left, right, contract):
    return lax.psum_scatter(
        lax.dot_general(
            left, right, (((1,), (contract,)), ((), ())), preferred_element_type=jnp.float32
        ).astype(jnp.bfloat16),
        "tensor",
        scatter_dimension=0,
        tiled=True,
    ).astype(jnp.float32)


def block_scores(query_block, keys, start, slopes, segments):
    rows = query_block.shape[0]
    scores = jnp.einsum(
        "qhd,khd->hqk", query_block, keys, preferred_element_type=jnp.float32
    ) * HD ** (-0.5)
    row_place = start + jnp.arange(rows)
    key_place = jnp.arange(keys.shape[0])
    distance = (row_place[:, None] - key_place[None, :]).astype(jnp.float32)
    scores = scores - slopes[:, None, None] * distance[None]
    row_segments = lax.dynamic_slice_in_dim(segments, start, rows)
    allowed = (row_segments[:, None] == segments[None, :]) & (
        key_place[None, :] <= row_place[:, None]
    )
    return jnp.where(allowed[None], scores, -1e30)


def attend_forward(query, keys, values, slopes, segments):
    total = query.shape[0]
    rows = min(512, total)

    def one_block(index):
        start = index * rows
        query_block = lax.dynamic_slice_in_dim(query, start, rows)
        scores = block_scores(query_block, keys, start, slopes, segments)
        top = jnp.max(scores, axis=-1, keepdims=True)
        weights = jnp.exp(scores - top)
        weight_sum = jnp.sum(weights, axis=-1, keepdims=True)
        probs = (weights / weight_sum).astype(jnp.bfloat16)
        heads = jnp.einsum("hqk,khd->qhd", probs, values, preferred_element_type=jnp.float32)
        return (heads, top[..., 0] + jnp.log(weight_sum[..., 0]))

    heads, logsum = lax.map(one_block, jnp.arange(total // rows))
    return (heads.reshape(total, -1), logsum)


def attend_backward(query, keys, values, slopes, segments, logsum, heads_grad):
    total = query.shape[0]
    rows = min(512, total)
    scale = HD ** (-0.5)

    def one_block(carry, index):
        key_grad, value_grad = carry
        start = index * rows
        query_block = lax.dynamic_slice_in_dim(query, start, rows)
        grad_block = lax.dynamic_slice_in_dim(heads_grad, start, rows)
        scores = block_scores(query_block, keys, start, slopes, segments)
        probs = jnp.exp(scores - logsum[index][..., None])
        prob_grad = jnp.einsum(
            "qhd,khd->hqk", grad_block, values, preferred_element_type=jnp.float32
        )
        inner_sum = jnp.sum(probs * prob_grad, axis=-1, keepdims=True)
        score_grad = (probs * (prob_grad - inner_sum)).astype(jnp.bfloat16)
        query_grad = (
            jnp.einsum("hqk,khd->qhd", score_grad, keys, preferred_element_type=jnp.float32) * scale
        )
        key_grad = (
            key_grad
            + jnp.einsum(
                "hqk,qhd->khd", score_grad, query_block, preferred_element_type=jnp.float32
            )
            * scale
        )
        value_grad = value_grad + jnp.einsum(
            "hqk,qhd->khd",
            probs.astype(jnp.bfloat16),
            grad_block,
            preferred_element_type=jnp.float32,
        )
        return ((key_grad, value_grad), query_grad)

    zeros = jnp.zeros(keys.shape, jnp.float32)
    (key_grad, value_grad), query_grad = lax.scan(
        one_block, (zeros, zeros), jnp.arange(total // rows)
    )
    return (
        query_grad.reshape(total, -1),
        key_grad.reshape(total, -1),
        value_grad.reshape(total, -1),
    )


def on_device(
    tokens,
    segments,
    norm_gains,
    norm_biases,
    qkv_weight,
    qv_bias,
    out_weight,
    out_bias,
    up_weight,
    up_bias,
    down_weight,
    down_bias,
    out_grad,
):

    def fetch_attention():
        return (
            lax.all_gather(norm_gains, "dp", axis=1, tiled=True),
            lax.all_gather(norm_biases, "dp", axis=1, tiled=True),
            lax.all_gather(qkv_weight, "dp", axis=0, tiled=True),
            lax.all_gather(qv_bias, "dp", axis=1, tiled=True),
            lax.all_gather(out_weight, "dp", axis=1, tiled=True),
            lax.all_gather(out_bias, "dp", axis=0, tiled=True),
        )

    def fetch_mlp():
        return (
            lax.all_gather(up_weight, "dp", axis=0, tiled=True),
            lax.all_gather(up_bias, "dp", axis=1, tiled=True),
            lax.all_gather(down_weight, "dp", axis=1, tiled=True),
            lax.all_gather(down_bias, "dp", axis=0, tiled=True),
        )

    gain_low, shift_low, qkv_full, qv_full, out_full, out_shift = fetch_attention()
    gain_rows = gain_low.astype(jnp.float32)
    shift_rows = shift_low.astype(jnp.float32)
    local_width = qkv_full.shape[2]
    local_heads = local_width // HD
    slopes = head_slopes(local_heads)
    inputs = tokens.astype(jnp.float32)
    normed = norm_rows(inputs, gain_rows[0], shift_rows[0]).astype(jnp.bfloat16)
    normed_all = gather_rows(normed)
    total = normed_all.shape[0]
    mixed = jnp.dot(
        normed_all, qkv_full.reshape(D, 3 * local_width), preferred_element_type=jnp.float32
    ).reshape(total, 3, local_width)
    query = (
        (mixed[:, 0] + qv_full[:, :HD].reshape(local_width))
        .astype(jnp.bfloat16)
        .reshape(total, local_heads, HD)
    )
    keys = mixed[:, 1].astype(jnp.bfloat16).reshape(total, local_heads, HD)
    values = (
        (mixed[:, 2] + qv_full[:, HD:].reshape(local_width))
        .astype(jnp.bfloat16)
        .reshape(total, local_heads, HD)
    )
    heads, logsum = attend_forward(query, keys, values, slopes, segments)
    heads = heads.astype(jnp.bfloat16)
    projected = spread_rows(heads, out_full, 0)
    middle = inputs + projected + out_shift.astype(jnp.float32)
    up_full, up_shift, down_full, down_shift = fetch_mlp()
    normed_mid = norm_rows(middle, gain_rows[1], shift_rows[1]).astype(jnp.bfloat16)
    mid_all = gather_rows(normed_mid)
    inner = jnp.dot(mid_all, up_full, preferred_element_type=jnp.float32) + up_shift.reshape(
        -1
    ).astype(jnp.float32)
    active = jax.nn.gelu(inner, approximate=True).astype(jnp.bfloat16)
    output = (middle + spread_rows(active, down_full, 0) + down_shift.astype(jnp.float32)).astype(
        jnp.bfloat16
    )
    refetched = fetch_mlp()
    up_full = refetched[0]
    down_full = refetched[2]
    grad_all = gather_rows(out_grad)
    down_grad = lax.dot_general(
        active, grad_all, (((0,), (0,)), ((), ())), preferred_element_type=jnp.float32
    )
    down_shift_grad = jnp.sum(grad_all, axis=0, dtype=jnp.float32)
    active_grad = lax.dot_general(
        grad_all, down_full, (((1,), (1,)), ((), ())), preferred_element_type=jnp.float32
    )
    inner_grad = jax.vjp(partial(jax.nn.gelu, approximate=True), inner)[1](active_grad)[0].astype(
        jnp.bfloat16
    )
    up_grad = lax.dot_general(
        mid_all, inner_grad, (((0,), (0,)), ((), ())), preferred_element_type=jnp.float32
    )
    up_shift_grad = jnp.sum(inner_grad, axis=0, dtype=jnp.float32).reshape(up_shift.shape)
    mid_norm_grad = spread_rows(inner_grad, up_full, 1)
    middle_back, gain_mid, shift_mid = jax.vjp(norm_rows, middle, gain_rows[1], shift_rows[1])[1](
        mid_norm_grad
    )
    middle_grad = out_grad.astype(jnp.float32) + middle_back
    up_sum, up_shift_sum, down_sum, down_shift_sum = (
        lax.psum_scatter(up_grad, "dp", scatter_dimension=0, tiled=True),
        lax.psum_scatter(up_shift_grad, "dp", scatter_dimension=1, tiled=True),
        lax.psum_scatter(down_grad, "dp", scatter_dimension=1, tiled=True),
        lax.psum_scatter(down_shift_grad, "dp", scatter_dimension=0, tiled=True),
    )
    refetched_attention = fetch_attention()
    qkv_full = refetched_attention[2]
    out_full = refetched_attention[4]
    middle_low = middle_grad.astype(jnp.bfloat16)
    middle_all = gather_rows(middle_low)
    out_weight_grad = lax.dot_general(
        heads, middle_all, (((0,), (0,)), ((), ())), preferred_element_type=jnp.float32
    )
    out_shift_grad = jnp.sum(middle_all, axis=0, dtype=jnp.float32)
    heads_grad = lax.dot_general(
        middle_all, out_full, (((1,), (1,)), ((), ())), preferred_element_type=jnp.float32
    )
    heads_grad = heads_grad.astype(jnp.bfloat16).reshape(total, local_heads, HD)
    query_grad, key_grad, value_grad = attend_backward(
        query, keys, values, slopes, segments, logsum, heads_grad
    )
    mixed_grad = jnp.stack([query_grad, key_grad, value_grad], axis=1).astype(jnp.bfloat16)
    flat_grad = mixed_grad.reshape(total, 3 * local_width)
    qkv_grad = lax.dot_general(
        normed_all, flat_grad, (((0,), (0,)), ((), ())), preferred_element_type=jnp.float32
    ).reshape(D, 3, local_width)
    column_sums = jnp.sum(mixed_grad, axis=0, dtype=jnp.float32)
    qv_grad = jnp.concatenate(
        [column_sums[0].reshape(local_heads, HD), column_sums[2].reshape(local_heads, HD)], axis=1
    )
    normed_grad = spread_rows(flat_grad, qkv_full.reshape(D, 3 * local_width), 1)
    input_back, gain_first, shift_first = jax.vjp(norm_rows, inputs, gain_rows[0], shift_rows[0])[
        1
    ](normed_grad)
    input_grad = middle_grad + input_back
    gain_grads = jnp.stack([gain_first, gain_mid])
    shift_grads = jnp.stack([shift_first, shift_mid])
    gain_part, shift_part, qkv_sum, qv_sum, out_weight_sum, out_shift_sum = (
        lax.psum_scatter(gain_grads, "dp", scatter_dimension=1, tiled=True),
        lax.psum_scatter(shift_grads, "dp", scatter_dimension=1, tiled=True),
        lax.psum_scatter(qkv_grad, "dp", scatter_dimension=0, tiled=True),
        lax.psum_scatter(qv_grad, "dp", scatter_dimension=1, tiled=True),
        lax.psum_scatter(out_weight_grad, "dp", scatter_dimension=1, tiled=True),
        lax.psum_scatter(out_shift_grad, "dp", scatter_dimension=0, tiled=True),
    )
    gain_sum, shift_sum = lax.psum((gain_part, shift_part), "tensor")
    return (
        output,
        input_grad,
        gain_sum,
        shift_sum,
        qkv_sum,
        qv_sum,
        out_weight_sum,
        out_shift_sum,
        up_sum,
        up_shift_sum,
        down_sum,
        down_shift_sum,
    )


def solution(mesh):
    placed = (
        P(("dp", "tensor"), None),
        P("dp"),
        P(None, "dp"),
        P(None, "dp"),
        P("dp", None, "tensor"),
        P("tensor", "dp"),
        P("tensor", "dp"),
        P("dp"),
        P("dp", "tensor"),
        P("tensor", "dp"),
        P("tensor", "dp"),
        P("dp"),
        P(("dp", "tensor"), None),
    )
    return jax.shard_map(
        on_device,
        mesh=mesh,
        in_specs=placed,
        out_specs=(
            P(("dp", "tensor"), None),
            P(("dp", "tensor"), None),
            P(None, "dp"),
            P(None, "dp"),
            P("dp", None, "tensor"),
            P("tensor", "dp"),
            P("tensor", "dp"),
            P("dp"),
            P("dp", "tensor"),
            P("tensor", "dp"),
            P("tensor", "dp"),
            P("dp"),
        ),
        check_vma=False,
    )
```

profile of v0, /device:TPU:0, one launch (start us, length us, event | category | flops | bytes accessed | tf_op | source)
XLA Modules:
  0.0 1474.4 jit_solution(8031347554438410817)
XLA Ops:
  8.0 22.3 %all_gather.46 = bf16[2,1024]{1,0:T(2,128)(2,1)S(1)} all-gather(bf16[2,128]{1,0:T(2,128)(2,1)} %param.19), channel_id=1, replica_groups=mesh['dp'=8,'tensor'=4] {'dp'}, dimensions={1}, use_global_device_ids=true | all-gather | bytes 4608 | tf_op jit(solution)/shard_map/all_gather | solution.py:142
  30.3 16.4 %all_gather.47 = bf16[2,1024]{1,0:T(2,128)(2,1)S(1)} all-gather(bf16[2,128]{1,0:T(2,128)(2,1)} %param.20), channel_id=1, replica_groups=mesh['dp'=8,'tensor'=4] {'dp'}, dimensions={1}, use_global_device_ids=true | all-gather | bytes 4608 | tf_op jit(solution)/shard_map/all_gather | solution.py:143
  54.4 18.2 %all-gather = bf16[8,16,4]{1,2,0:T(4,128)(2,1)S(1)} all-gather(bf16[1,16,4]{1,2,0:T(4,128)(2,1)S(1)} %bitcast.190), channel_id=1, replica_groups=mesh['dp'=8,'tensor'=4] {'dp'}, dimensions={0}, use_global_device_ids=true | all-gather | bytes 1152 | tf_op jit(solution)/shard_map/all_gather | solution.py:145
  72.7 28.8 %all_gather.51 = bf16[256,1024]{1,0:T(8,128)(2,1)} all-gather(bf16[256,128]{1,0:T(8,128)(2,1)S(1)} %copy-done.22), channel_id=1, replica_groups=mesh['dp'=8,'tensor'=4] {'dp'}, dimensions={1}, use_global_device_ids=true | all-gather | bytes 589824 | tf_op jit(solution)/shard_map/all_gather | solution.py:146
  111.9 95.2 %while.28 = (s32[]{:T(128)}, bf16[4,512,4,64]{1,3,2,0:T(8,128)(2,1)}, f32[4,4,512]{2,1,0:T(4,128)S(1)}, s32[4]{0:T(128)S(1)}, s32[2048]{0:T(1024)S(1)}, /*index=...) while((s32[]{:T(128)}, ...), condition=%wide.region_5.6_spmd.clone, body=%wide.region_2.5_spmd.clone.sunk | while | flops 1154480640 | bytes 91050288 | solution.py:74
  214.4 16.2 %all-gather.1 = bf16[8,1,128]{2,1,0:T(2,128)(2,1)S(1)} all-gather(bf16[1,1,128]{2,1,0:T(2,128)(2,1)S(1)} %bitcast.191), channel_id=1, replica_groups=mesh['dp'=8,'tensor'=4] {'dp'}, dimensions={0}, use_global_device_ids=true | all-gather | bytes 2304 | tf_op jit(solution)/shard_map/all_gather | solution.py:147
  230.6 25.7 %reduce-scatter.21.cloned.1.call-done = bf16[512,1024]{1,0:T(8,128)(2,1)} async-done(((bf16[2048,1024]{1,0:T(8,128)(2,1)}), bf16[512,1024]{1,0:T(8,128)(2,1)}) %reduce-scatter.21.cloned.1.call-update) | async-done | bytes 1048592 | tf_op jit(solution)/shard_map/reduce_scatter | solution.py:33
  262.9 26.2 %all-gather.2 = bf16[8,16,8]{1,2,0:T(8,128)(2,1)S(1)} all-gather(bf16[1,16,8]{1,2,0:T(8,128)(2,1)S(1)} %bitcast.189), channel_id=1, replica_groups=mesh['dp'=8,'tensor'=4] {'dp'}, dimensions={0}, use_global_device_ids=true | all-gather | bytes 2304 | tf_op jit(solution)/shard_map/all_gather | solution.py:153
  289.1 18.9 %all-gather.18.cloned.1.call-done = bf16[1024,1024]{1,0:T(8,128)(2,1)} async-done(((bf16[128,1024]{1,0:T(8,128)(2,1)}), bf16[1024,1024]{1,0:T(8,128)(2,1)}) %all-gather.18.cloned.1.call-update) | async-done | bytes 2097168 | tf_op jit(solution)/shard_map/all_gather | solution.py:152
  308.0 35.1 %all-gather.16.cloned.1.call-done = bf16[2048,1024]{1,0:T(8,128)(2,1)} async-done(((bf16[512,1024]{1,0:T(8,128)(2,1)}), bf16[2048,1024]{1,0:T(8,128)(2,1)}) %all-gather.16.cloned.1.call-update) | async-done | bytes 4194320 | tf_op jit(solution)/shard_map/all_gather | solution.py:29
  353.7 42.6 %all-gather.20.cloned.1.call-done = bf16[1024,1024]{1,0:T(8,128)(2,1)} async-done(((bf16[1024,128]{1,0:T(8,128)(2,1)}), bf16[1024,1024]{1,0:T(8,128)(2,1)}) %all-gather.20.cloned.1.call-update) | async-done | bytes 2097168 | tf_op jit(solution)/shard_map/all_gather | solution.py:154
  396.3 34.3 %all-gather.22.cloned.1.call-done = bf16[2048,1024]{1,0:T(8,128)(2,1)} async-done(((bf16[512,1024]{1,0:T(8,128)(2,1)}), bf16[2048,1024]{1,0:T(8,128)(2,1)}) %all-gather.22.cloned.1.call-update) | async-done | bytes 4194320 | tf_op jit(solution)/shard_map/all_gather | solution.py:29
  430.7 14.6 convert_reduce_fusion.1
  466.4 20.4 %all-gather.3 = bf16[8,1,128]{2,1,0:T(2,128)(2,1)S(1)} all-gather(bf16[1,1,128]{2,1,0:T(2,128)(2,1)S(1)} %bitcast.192), channel_id=1, replica_groups=mesh['dp'=8,'tensor'=4] {'dp'}, dimensions={0}, use_global_device_ids=true | all-gather | bytes 2304 | tf_op jit(solution)/shard_map/all_gather | solution.py:155
  501.1 44.2 %reduce-scatter.23.cloned.1.call-done = bf16[512,1024]{1,0:T(8,128)(2,1)} async-done(((bf16[2048,1024]{1,0:T(8,128)(2,1)}), bf16[512,1024]{1,0:T(8,128)(2,1)}) %reduce-scatter.23.cloned.1.call-update) | async-done | bytes 1048592 | tf_op jit(solution)/shard_map/reduce_scatter | solution.py:33
  551.8 34.6 %all-gather.24.cloned.1.call-done = bf16[2048,1024]{1,0:T(8,128)(2,1)} async-done(((bf16[512,1024]{1,0:T(8,128)(2,1)}), bf16[2048,1024]{1,0:T(8,128)(2,1)}) %all-gather.24.cloned.1.call-update) | async-done | bytes 4194320 | tf_op jit(solution)/shard_map/all_gather | solution.py:29
  591.9 222.2 %while.29 = (s32[]{:T(128)}, f32[2048,4,64]{0,2,1:T(8,128)}, f32[2048,4,64]{0,2,1:T(8,128)}, bf16[4,512,4,64]{1,3,2,0:T(8,128)(2,1)}, s32[4]{0:T(128)S(1)}, /*in...) while((s32[]{:T(128)}, f32[2048,4,64]{0,2,1:T(8,128)}, ...), condition=%wide.region_15.16_spmd.clone, body=%wide.region_13.15_spmd.clone.sunk | while | flops 2738485760 | bytes 216592752 | solution.py:114
  606.0 14.1 multiply_reduce_fusion.3
  660.4 14.1 multiply_reduce_fusion.3
  716.2 14.1 multiply_reduce_fusion.3
  772.1 14.1 multiply_reduce_fusion.3
  837.6 42.2 %reduce-scatter.27.cloned.1.call-done = bf16[512,1024]{1,0:T(8,128)(2,1)} async-done(((bf16[2048,1024]{1,0:T(8,128)(2,1)}), bf16[512,1024]{1,0:T(8,128)(2,1)}) %reduce-scatter.27.cloned.1.call-update) | async-done | bytes 1048592 | tf_op jit(solution)/shard_map/reduce_scatter | solution.py:33
  886.5 12.6 fusion.72
  932.6 11.8 reduce-scatter.43.cloned.1.call-done
  948.6 19.7 %all-reduce.2 = (f32[1024]{0:T(1024)S(1)}, f32[1024]{0:T(1024)S(1)}) all-reduce(f32[1024]{0:T(1024)S(1)} %convert_reduce_fusion.2, f32[1024]{0:T(1024)S(1)} %convert_reduce_fusion), channel_id=11, replica_groups=mesh['dp'=8,'tensor'=4] {'dp'}, use_global_device_ids=true, to_apply=%region_32.33.clone | all-reduce | flops 2048 | bytes 16384
  969.5 39.1 %reduce-scatter.41.cloned.1.call-done = f32[16,4]{1,0:T(8,128)} async-done(((f32[128,4]{1,0:T(8,128)}), f32[16,4]{1,0:T(8,128)}) %reduce-scatter.41.cloned.1.call-update) | async-done | bytes 272
  1013.8 59.0 %reduce-scatter.37.cloned.1.call-done = f32[128,2]{1,0:T(8,128)} async-done(((f32[1024,2]{1,0:T(8,128)}), f32[128,2]{1,0:T(8,128)}) %reduce-scatter.37.cloned.1.call-update) | async-done | bytes 1040
  1073.7 63.5 %reduce-scatter.39.cloned.1.call-done = f32[128,2]{1,0:T(8,128)} async-done(((f32[1024,2]{1,0:T(8,128)}), f32[128,2]{1,0:T(8,128)}) %reduce-scatter.39.cloned.1.call-update) | async-done | bytes 1040
  1144.4 84.5 %reduce-scatter.35.cloned.1.call-done = f32[1024,128]{1,0:T(8,128)} async-done(((f32[1024,1024]{1,0:T(8,128)}), f32[1024,128]{1,0:T(8,128)}) %reduce-scatter.35.cloned.1.call-update) | async-done | bytes 524304 | tf_op jit(solution)/shard_map/reduce_scatter | solution.py:222
  1228.9 92.4 %reduce-scatter.33.cloned.1.call-done = f32[128,1024]{1,0:T(8,128)} async-done(((f32[1024,1024]{1,0:T(8,128)}), f32[128,1024]{1,0:T(8,128)}) %reduce-scatter.33.cloned.1.call-update) | async-done | bytes 524304 | tf_op jit(solution)/shard_map/reduce_scatter | solution.py:220
  1321.3 67.6 %reduce-scatter.31.cloned.1.call-done = f32[256,128]{1,0:T(8,128)} async-done(((f32[256,1024]{1,0:T(8,128)}), f32[256,128]{1,0:T(8,128)}) %reduce-scatter.31.cloned.1.call-update) | async-done | bytes 131088 | tf_op jit(solution)/shard_map/reduce_scatter | solution.py:262
  1388.9 78.5 %reduce-scatter.29.cloned.1.call-done = f32[128,3,256]{2,0,1:T(8,128)} async-done(((f32[1024,3,256]{2,0,1:T(8,128)}), f32[128,3,256]{2,0,1:T(8,128)}) %reduce-scatter.29.cloned.1.call-update) | async-done | bytes 393232 | tf_op jit(solution)/shard_map/reduce_scatter | solution.py:260
  (303 shorter events, 419.2 us)
Async XLA Ops:
  7.2 47.2 %copy-start.36 = (bf16[4,16]{1,0:T(4,128)(2,1)S(1)}, bf16[4,16]{1,0:T(4,128)(2,1)}, u32[]{:S(2)}) copy-start(bf16[4,16]{1,0:T(4,128)(2,1)} %param.22) | copy-start | bytes 388
  7.2 65.6 %copy-start.22 = (bf16[256,128]{1,0:T(8,128)(2,1)S(1)}, bf16[256,128]{1,0:T(8,128)(2,1)}, u32[]{:S(2)}) copy-start(bf16[256,128]{1,0:T(8,128)(2,1)} %param.23) | copy-start | bytes 196612
  7.2 94.3 %all-gather.14.cloned.1.call-start = ((), (), s32[]{:S(2)}) async-start(), calls=%async_computation.13 | async-start | bytes 1769472 | tf_op jit(solution)/shard_map/all_gather | solution.py:144
  7.9 95.3 %all-gather.12.cloned.1.call-start = ((), (), s32[]{:S(2)}) async-start(), calls=%async_computation.12 | async-start | bytes 5242880 | tf_op jit(solution)/shard_map/all_gather | solution.py:29
  54.3 202.0 %reduce-scatter.21.cloned.1.call-start = ((), (), s32[]{:S(2)}) async-start(), calls=%async_computation.14 | async-start | bytes 5242880 | tf_op jit(solution)/shard_map/reduce_scatter | solution.py:33
  213.8 46.1 %copy-start.21 = (f32[1,1024]{1,0:T(1,128)S(1)}, f32[1,1024]{1,0:T(1,128)}, u32[]{:S(2)}) copy-start(f32[1,1024]{1,0:T(1,128)} %get-tuple-element.261) | copy-start | bytes 12292
  213.8 46.1 %copy-start.31 = (f32[1,1024]{1,0:T(1,128)S(1)}, f32[1,1024]{1,0:T(1,128)}, u32[]{:S(2)}) copy-start(f32[1,1024]{1,0:T(1,128)} %get-tuple-element.263) | copy-start | bytes 12292
  213.8 94.2 %all-gather.18.cloned.1.call-start = ((), (), s32[]{:S(2)}) async-start(), calls=%async_computation.16 | async-start | bytes 2359296 | tf_op jit(solution)/shard_map/all_gather | solution.py:152
  214.4 128.7 %all-gather.16.cloned.1.call-start = ((), (), s32[]{:S(2)}) async-start(), calls=%async_computation.15 | async-start | bytes 5242880 | tf_op jit(solution)/shard_map/all_gather | solution.py:29
  261.5 134.8 %all-gather.20.cloned.1.call-start = ((), (), s32[]{:S(2)}) async-start(), calls=%async_computation.17 | async-start | bytes 2359296 | tf_op jit(solution)/shard_map/all_gather | solution.py:154
  262.0 168.6 %all-gather.22.cloned.1.call-start = ((), (), s32[]{:S(2)}) async-start(), calls=%async_computation.19 | async-start | bytes 5242880 | tf_op jit(solution)/shard_map/all_gather | solution.py:29
  262.8 235.4 %reduce-scatter.25.cloned.1.call-start = ((), (), s32[]{:S(2)}) async-start(), calls=%async_computation.20 | async-start | bytes 5242880 | tf_op jit(solution)/shard_map/reduce_scatter | solution.py:33
  289.1 164.9 %copy-start.32 = (f32[128,8]{0,1:T(8,128)}, f32[128,8]{0,1:T(8,128)S(1)}, u32[]{:S(2)}) copy-start(f32[128,8]{0,1:T(8,128)S(1)} %reshape.332) | copy-start | bytes 12292
  453.5 91.8 %reduce-scatter.23.cloned.1.call-start = ((), (), s32[]{:S(2)}) async-start(), calls=%async_computation.18 | async-start | bytes 5242880 | tf_op jit(solution)/shard_map/reduce_scatter | solution.py:33
  465.8 120.6 %all-gather.24.cloned.1.call-start = ((), (), s32[]{:S(2)}) async-start(), calls=%async_computation.21 | async-start | bytes 5242880 | tf_op jit(solution)/shard_map/all_gather | solution.py:29
  551.7 328.1 %reduce-scatter.27.cloned.1.call-start = ((), (), s32[]{:S(2)}) async-start(), calls=%async_computation.22 | async-start | bytes 5242880 | tf_op jit(solution)/shard_map/reduce_scatter | solution.py:33
  835.1 44.8 %copy-start.20 = (f32[512]{0:T(512)S(1)}, f32[512]{0:T(512)}, u32[]{:S(2)}) copy-start(f32[512]{0:T(512)} %copy-done.19) | copy-start | bytes 6148
  835.1 46.7 %copy-start.28 = (f32[512]{0:T(512)S(1)}, f32[512]{0:T(512)}, u32[]{:S(2)}) copy-start(f32[512]{0:T(512)} %copy-done.27) | copy-start | bytes 6148
  835.1 46.7 %copy-start.24 = (f32[512]{0:T(512)S(1)}, f32[512]{0:T(512)}, u32[]{:S(2)}) copy-start(f32[512]{0:T(512)} %copy-done.23) | copy-start | bytes 6148
  835.1 49.1 %copy-start.30 = (f32[1024]{0:T(1024)S(1)}, f32[1024]{0:T(1024)}, u32[]{:S(2)}) copy-start(f32[1024]{0:T(1024)} %get-tuple-element.192) | copy-start | bytes 12292
  835.1 50.2 %copy-start.29 = (f32[1024]{0:T(1024)S(1)}, f32[1024]{0:T(1024)}, u32[]{:S(2)}) copy-start(f32[1024]{0:T(1024)} %get-tuple-element.198) | copy-start | bytes 12292
  835.2 51.4 %copy-start.33 = (f32[128,8]{0,1:T(8,128)S(1)}, f32[128,8]{0,1:T(8,128)}, u32[]{:S(2)}) copy-start(f32[128,8]{0,1:T(8,128)} %copy-done.32) | copy-start | bytes 12292
  835.2 109.2 %reduce-scatter.43.cloned.1.call-start = ((), (), s32[]{:S(2)}) async-start(), calls=%async_computation.30 | async-start | bytes 73728
  836.5 172.2 %reduce-scatter.41.cloned.1.call-start = ((), (), s32[]{:S(2)}) async-start(), calls=%async_computation.29 | async-start | bytes 73728
  837.6 235.2 %reduce-scatter.37.cloned.1.call-start = ((), (), s32[]{:S(2)}) async-start(), calls=%async_computation.27 | async-start | bytes 589824
  885.3 252.0 %reduce-scatter.39.cloned.1.call-start = ((), (), s32[]{:S(2)}) async-start(), calls=%async_computation.28 | async-start | bytes 589824
  886.5 342.5 %reduce-scatter.35.cloned.1.call-start = ((), (), s32[]{:S(2)}) async-start(), calls=%async_computation.26 | async-start | bytes 4718592 | tf_op jit(solution)/shard_map/reduce_scatter | solution.py:222
  899.1 422.2 %reduce-scatter.33.cloned.1.call-start = ((), (), s32[]{:S(2)}) async-start(), calls=%async_computation.25 | async-start | bytes 4718592 | tf_op jit(solution)/shard_map/reduce_scatter | solution.py:220
  909.5 479.4 %reduce-scatter.31.cloned.1.call-start = ((), (), s32[]{:S(2)}) async-start(), calls=%async_computation.24 | async-start | bytes 1179648 | tf_op jit(solution)/shard_map/reduce_scatter | solution.py:262
  915.2 552.2 %reduce-scatter.29.cloned.1.call-start = ((), (), s32[]{:S(2)}) async-start(), calls=%async_computation.23 | async-start | bytes 3538944 | tf_op jit(solution)/shard_map/reduce_scatter | solution.py:260
  929.6 80.5 %copy-start.8 = (f32[512,1024]{1,0:T(8,128)S(1)}, f32[512,1024]{1,0:T(8,128)}, u32[]{:S(2)}) copy-start(f32[512,1024]{1,0:T(8,128)} %copy-done.7) | copy-start | bytes 6291460
  929.6 80.5 %copy-start.26 = (f32[512]{0:T(512)S(1)}, f32[512]{0:T(512)}, u32[]{:S(2)}) copy-start(f32[512]{0:T(512)} %copy-done.25) | copy-start | bytes 6148
  (35 other events, 412.3 us)
Sparse Core Ops, SparseCore 0:
  10.2 46.6 all-gather.13
  59.1 33.2 all-gather.11
  213.9 42.3 reduce-scatter.20
  258.5 49.4 all-gather.17
  310.1 32.9 all-gather.15
  345.2 51.0 all-gather.19
  398.0 32.6 all-gather.21
  453.7 44.5 reduce-scatter.24
  500.7 44.5 reduce-scatter.22
  551.9 34.4 all-gather.23
  835.3 44.5 reduce-scatter.26
  883.1 61.2 reduce-scatter.42
  948.4 60.2 reduce-scatter.40
  1011.9 60.9 reduce-scatter.36
  1076.4 60.8 reduce-scatter.38
  1141.3 87.5 reduce-scatter.34
  1233.4 87.8 reduce-scatter.32
  1325.1 63.7 reduce-scatter.30
  1393.5 73.8 reduce-scatter.28
where the time goes:
time: 1480 us; the launch traced here: 1470 us
  waiting for transfers between devices  788 us (53%)
  matrix products  298 us (20%)
  blocking collectives  174 us (12%)
  other arithmetic  118 us (8%)
  local copies, waits for them, and re-layouts  64.8 us (4%)
  between operations  15.6 us (1%)
    unnamed x23, waiting for transfers between devices  176 us
    reduce_scatter x4, waiting for transfers between devices, spread_rows(): lax.psum_scatter(lax.dot_general(left, right, (((1,), (contract,)), ((),...  123 us
    all_gather x4, waiting for transfers between devices, gather_rows(): return lax.all_gather(values, 'tensor', axis=0, tiled=True)  104 us
    reduce_scatter x1, waiting for transfers between devices, on_device(): lax.psum_scatter(up_grad, 'dp', scatter_dimension=0, tiled=True)  92.4 us
    reduce_scatter x1, waiting for transfers between devices, on_device(): lax.psum_scatter(down_grad, 'dp', scatter_dimension=1, tiled=True)  84.5 us
    dot_general x8, matrix products, block_scores(): jnp.einsum('qhd,khd->hqk', query_block, keys, preferred_element_type=jnp....  81.7 us
    reduce_scatter x1, waiting for transfers between devices, on_device(): lax.psum_scatter(qkv_grad, 'dp', scatter_dimension=0, tiled=True)  78.5 us
    reduce_scatter x1, waiting for transfers between devices, on_device(): lax.psum_scatter(out_weight_grad, 'dp', scatter_dimension=1, tiled=True)  67.6 us
  transfers between devices with their start and end apart: 19, of which 17 were waited for; matrix products, arithmetic and copies ran while one was open for 7% of the time, Pallas kernels for 0%

commit v1 on v0

v1 whole, which is shorter than its diff:
```python
import jax
import jax.numpy as jnp
from jax import lax
from jax.experimental import pallas as pl
from jax.experimental.pallas import tpu as pltpu
from jax.sharding import PartitionSpec as P

D = 1024
H = 16
HD = 64
BLOCK = 256
LOG2E = 1.4426950408889634
EPS = 1e-05
F32 = jnp.float32
LOW = jnp.bfloat16


def norm_rows(values, gain, shift):
    centre = jnp.mean(values, axis=-1, keepdims=True)
    centred = values - centre
    spread = jnp.mean(centred * centred, axis=-1, keepdims=True)
    return centred * lax.rsqrt(spread + EPS) * gain + shift


def standard_rows(values):
    centre = jnp.mean(values, axis=-1, keepdims=True)
    centred = values - centre
    spread = jnp.mean(centred * centred, axis=-1, keepdims=True)
    return centred * lax.rsqrt(spread + EPS)


def dot(left, right, left_dim, right_dim):
    return lax.dot_general(
        left, right, (((left_dim,), (right_dim,)), ((), ())), preferred_element_type=F32
    )


def swap(value, bit, size):
    return lax.ppermute(value, "tensor", [(place, place ^ bit) for place in range(size)])


def gather_blocks(own, size):
    blocks = [own]
    if size == 4:
        far = swap(own, 2, size)
        near = swap(own, 1, size)
        return [own, near, far, swap(far, 1, size)]
    for bit in range(1, size):
        blocks.append(swap(own, bit, size))
    return blocks


def spread_blocks(term, size):
    if size == 4:
        across = swap(term(3).astype(LOW), 1, size)
        partner = term(2) + across.astype(F32)
        partner = swap(partner.astype(LOW), 2, size)
        beside = swap(term(1).astype(LOW), 1, size)
        return term(0) + beside.astype(F32) + partner.astype(F32)
    total = term(0)
    for bit in range(1, size):
        total = total + swap(term(bit).astype(LOW), bit, size).astype(F32)
    return total


def column_of(index):
    return slice(index * HD, (index + 1) * HD)


def tile_mask(iota, start_row, place_row, offset):
    return (iota >= start_row - offset) & (iota <= place_row - offset)


def forward_kernel(first_ref, clear_ref, phys_ref, slope_ref, start_ref, q_ref, k_ref, v_ref,
                   out_ref, lse_ref, vt_ref, bias_ref):
    i = pl.program_id(0)
    heads = q_ref.shape[1] // HD
    count = q_ref.shape[0] // BLOCK
    tile = (BLOCK, BLOCK)

    @pl.when(i == 0)
    def _():
        rows = lax.broadcasted_iota(jnp.int32, tile, 0).astype(F32)
        for h in range(heads):
            bias_ref[h] = rows * slope_ref[h]
        for b in range(count):
            block = v_ref[b * BLOCK : (b + 1) * BLOCK, :].astype(F32)
            vt_ref[b] = block.T.astype(LOW)

    here = pl.multiple_of(phys_ref[i] * BLOCK, BLOCK)
    q_block = q_ref[pl.ds(here, BLOCK), :]
    start_row = start_ref[i]
    place_row = i * BLOCK + lax.broadcasted_iota(jnp.int32, (1, BLOCK), 1)
    iota = lax.broadcasted_iota(jnp.int32, tile, 0)

    def step(masked, j, carry):
        there = pl.multiple_of(phys_ref[j] * BLOCK, BLOCK)
        k_block = k_ref[pl.ds(there, BLOCK), :]
        vt_block = vt_ref[phys_ref[j]]
        distance = ((j - i) * BLOCK).astype(F32)
        if masked:
            allowed = tile_mask(iota, start_row, place_row, j * BLOCK)
        result = []
        for h in range(heads):
            top, total, acc = carry[h]
            s = dot(k_block[:, column_of(h)], q_block[:, column_of(h)], 1, 1)
            s = s * (HD**-0.5 * LOG2E) + bias_ref[h]
            if masked:
                s = jnp.where(allowed, s, -1e30)
            off = slope_ref[h] * distance
            new_top = jnp.maximum(top, jnp.max(s, axis=0, keepdims=True) + off)
            p = jnp.exp2(s - (new_top - off))
            keep = jnp.exp2(top - new_top)
            total = total * keep + jnp.sum(p, axis=0, keepdims=True)
            acc = acc * keep + dot(vt_block[column_of(h), :], p.astype(LOW), 1, 0)
            result.append((new_top, total, acc))
        return tuple(result)

    carry = tuple(
        (
            jnp.full((1, BLOCK), -1e30, F32),
            jnp.zeros((1, BLOCK), F32),
            jnp.zeros((HD, BLOCK), F32),
        )
        for _ in range(heads)
    )
    carry = lax.fori_loop(first_ref[i], clear_ref[i], lambda j, c: step(True, j, c), carry)
    carry = lax.fori_loop(clear_ref[i], i, lambda j, c: step(False, j, c), carry)
    carry = step(True, i, carry)
    lse_ref[i] = jnp.concatenate([top + jnp.log2(total) for top, total, _ in carry], axis=0)
    flat = jnp.concatenate([acc / total for _, total, acc in carry], axis=0)
    out_ref[pl.ds(here, BLOCK), :] = flat.T.astype(LOW)


def backward_kernel(first_ref, clear_ref, phys_ref, slope_ref, start_ref, q_ref, k_ref, v_ref,
                    out_ref, grad_ref, lse_ref, dq_ref, dk_ref, dv_ref,
                    kt_ref, bias_ref, dk_sum, dv_sum):
    i = pl.program_id(0)
    heads = q_ref.shape[1] // HD
    count = q_ref.shape[0] // BLOCK
    tile = (BLOCK, BLOCK)

    @pl.when(i == 0)
    def _():
        rows = lax.broadcasted_iota(jnp.int32, tile, 0).astype(F32)
        for h in range(heads):
            bias_ref[h] = rows * slope_ref[h]
        for b in range(count):
            block = k_ref[b * BLOCK : (b + 1) * BLOCK, :].astype(F32)
            kt_ref[b] = block.T.astype(LOW)
        dk_sum[...] = jnp.zeros_like(dk_sum)
        dv_sum[...] = jnp.zeros_like(dv_sum)

    here = pl.multiple_of(phys_ref[i] * BLOCK, BLOCK)
    q_block = q_ref[pl.ds(here, BLOCK), :]
    g_block = grad_ref[pl.ds(here, BLOCK), :]
    product = (g_block.astype(F32) * out_ref[pl.ds(here, BLOCK), :].astype(F32)).T
    start_row = start_ref[i]
    place_row = i * BLOCK + lax.broadcasted_iota(jnp.int32, (1, BLOCK), 1)
    iota = lax.broadcasted_iota(jnp.int32, tile, 0)
    lse = lse_ref[i]
    inner = [jnp.sum(product[column_of(h), :], axis=0, keepdims=True) for h in range(heads)]

    def step(masked, j, carry):
        rows = pl.ds(pl.multiple_of(phys_ref[j] * BLOCK, BLOCK), BLOCK)
        k_block = k_ref[rows, :]
        v_block = v_ref[rows, :]
        kt_block = kt_ref[phys_ref[j]]
        distance = ((j - i) * BLOCK).astype(F32)
        if masked:
            allowed = tile_mask(iota, start_row, place_row, j * BLOCK)
        result = []
        for h in range(heads):
            s = dot(k_block[:, column_of(h)], q_block[:, column_of(h)], 1, 1)
            s = s * (HD**-0.5 * LOG2E) + bias_ref[h]
            p = jnp.exp2(s - (lse[h : h + 1, :] - slope_ref[h] * distance))
            if masked:
                p = jnp.where(allowed, p, 0.0)
            dp = dot(v_block[:, column_of(h)], g_block[:, column_of(h)], 1, 1)
            ds = (p * (dp - inner[h])).astype(LOW)
            dv_sum[h, rows, :] += dot(p.astype(LOW), g_block[:, column_of(h)], 1, 0)
            dk_sum[h, rows, :] += dot(ds, q_block[:, column_of(h)], 1, 0)
            result.append(carry[h] + dot(kt_block[column_of(h), :], ds, 1, 0))
        return tuple(result)

    carry = tuple(jnp.zeros((HD, BLOCK), F32) for _ in range(heads))
    carry = lax.fori_loop(first_ref[i], clear_ref[i], lambda j, c: step(True, j, c), carry)
    carry = lax.fori_loop(clear_ref[i], i, lambda j, c: step(False, j, c), carry)
    carry = step(True, i, carry)
    flat = jnp.concatenate(carry, axis=0) * HD**-0.5
    dq_ref[pl.ds(here, BLOCK), :] = flat.T.astype(LOW)

    @pl.when(i == count - 1)
    def _():
        for b in range(count):
            rows = slice(b * BLOCK, (b + 1) * BLOCK)
            dk_ref[rows, :] = (
                jnp.concatenate([dk_sum[h, rows, :] for h in range(heads)], axis=1) * HD**-0.5
            ).astype(LOW)
            dv_ref[rows, :] = jnp.concatenate(
                [dv_sum[h, rows, :] for h in range(heads)], axis=1
            ).astype(LOW)


SMEM = pl.BlockSpec(memory_space=pltpu.SMEM)
VMEM = pl.BlockSpec(memory_space=pltpu.VMEM)
LIMIT = 48 * 1024 * 1024


def attend_forward(plan, query, keys, values):
    total, width = query.shape
    heads, count = width // HD, total // BLOCK
    return pl.pallas_call(
        forward_kernel,
        grid=(count,),
        out_shape=(
            jax.ShapeDtypeStruct((total, width), LOW),
            jax.ShapeDtypeStruct((count, heads, BLOCK), F32),
        ),
        in_specs=[SMEM] * 4 + [VMEM] * 4,
        out_specs=(VMEM, VMEM),
        scratch_shapes=[
            pltpu.VMEM((count, width, BLOCK), LOW),
            pltpu.VMEM((heads, BLOCK, BLOCK), F32),
        ],
        compiler_params=pltpu.CompilerParams(vmem_limit_bytes=LIMIT),
        cost_estimate=pl.CostEstimate(
            flops=2 * total * total * width, bytes_accessed=8 * total * width,
            transcendentals=total * total * heads // 2),
        name="attend_forward",
    )(*plan, query, keys, values)


def attend_backward(plan, query, keys, values, heads_out, heads_grad, lse):
    total, width = query.shape
    heads, count = width // HD, total // BLOCK
    return pl.pallas_call(
        backward_kernel,
        grid=(count,),
        out_shape=(jax.ShapeDtypeStruct((total, width), LOW),) * 3,
        in_specs=[SMEM] * 4 + [VMEM] * 7,
        out_specs=(VMEM,) * 3,
        scratch_shapes=[
            pltpu.VMEM((count, width, BLOCK), LOW),
            pltpu.VMEM((heads, BLOCK, BLOCK), F32),
            pltpu.VMEM((heads, total, HD), F32),
            pltpu.VMEM((heads, total, HD), F32),
        ],
        compiler_params=pltpu.CompilerParams(vmem_limit_bytes=LIMIT),
        cost_estimate=pl.CostEstimate(
            flops=5 * total * total * width, bytes_accessed=16 * total * width,
            transcendentals=total * total * heads // 2),
        name="attend_backward",
    )(*plan, query, keys, values, heads_out, heads_grad, lse)


def attention_plan(segments, position, size, local_heads):
    total = segments.shape[0]
    count = total // BLOCK
    group = total // size // BLOCK
    place = jnp.arange(total, dtype=jnp.int32)
    fresh = jnp.concatenate([jnp.ones((1,), bool), segments[1:] != segments[:-1]])
    starts = lax.cummax(jnp.where(fresh, place, 0))
    block = jnp.arange(count, dtype=jnp.int32)
    first = starts[::BLOCK] // BLOCK
    clear = (starts[BLOCK - 1 :: BLOCK] + (BLOCK - 1)) // BLOCK
    clear = jnp.clip(clear, first, block)
    phys = ((block // group) ^ position) * group + block % group
    index = position * local_heads + jnp.arange(local_heads)
    slopes = 2.0 ** (-8.0 * (index.astype(F32) + 1.0) / H) * LOG2E
    return (first, clear, phys, slopes, starts.reshape(count, 1, BLOCK))


def on_device(tensor_size, dp_size):
    def run(tokens, segments, norm_gains, norm_biases, qkv_weight, qv_bias, out_weight, out_bias,
            up_weight, up_bias, down_weight, down_bias, out_grad):
        size = tensor_size
        position = lax.axis_index("tensor")
        part = D // dp_size
        local_width = qkv_weight.shape[2]
        local_heads = local_width // HD
        width = 3 * local_width

        token_blocks = gather_blocks(tokens, size)

        pieces = [norm_gains.reshape(-1), norm_biases.reshape(-1), out_bias, down_bias,
                  qv_bias.reshape(-1), up_bias.reshape(-1)]
        small = jnp.concatenate(pieces)
        extra = -(-small.shape[0] // (16 * width)) * 16
        small = jnp.pad(small, (0, extra * width - small.shape[0])).reshape(extra, width)
        packed = jnp.concatenate([qkv_weight.reshape(part, width), small], axis=0)
        packed = lax.all_gather(packed, "dp", axis=0)
        qkv_full = packed[:, :part].reshape(D, width)
        small = packed[:, part:].reshape(dp_size, -1)
        full = []
        place = 0
        for piece, shape in zip(
            pieces,
            (norm_gains.shape, norm_biases.shape, (1, part), (1, part), qv_bias.shape, up_bias.shape),
        ):
            block = small[:, place : place + piece.size].reshape((dp_size,) + shape)
            full.append(block.transpose(1, 0, 2).reshape(shape[0], -1).astype(F32))
            place += piece.size
        gain_rows, shift_rows, out_shift, down_shift, qv_full, up_shift = full
        out_full = lax.all_gather(out_weight, "dp", axis=1, tiled=True)
        up_full = lax.all_gather(up_weight, "dp", axis=0, tiled=True)
        down_full = lax.all_gather(down_weight, "dp", axis=1, tiled=True)
        grad_blocks = gather_blocks(out_grad, size)

        plan = attention_plan(segments, position, size, local_heads)
        inputs = tokens.astype(F32)
        normed = jnp.concatenate(
            [norm_rows(b.astype(F32), gain_rows[0], shift_rows[0]).astype(LOW)
             for b in token_blocks]
        )
        mixed_bias = jnp.concatenate(
            [qv_full[:, :HD].reshape(-1), jnp.zeros((local_width,), F32),
             qv_full[:, HD:].reshape(-1)]
        )
        mixed = (dot(normed, qkv_full, 1, 0) + mixed_bias).astype(LOW)
        query, keys, values = (
            mixed[:, c * local_width : (c + 1) * local_width] for c in range(3)
        )
        heads, lse = attend_forward(plan, query, keys, values)
        rows = tokens.shape[0]

        def block_of(array, r):
            return array[r * rows : (r + 1) * rows]

        projected = spread_blocks(lambda r: dot(block_of(heads, r), out_full, 1, 0), size)
        middle = inputs + projected + out_shift
        normed_mid = norm_rows(middle, gain_rows[1], shift_rows[1]).astype(LOW)
        mid_blocks = gather_blocks(normed_mid, size)

        active, inner_grad = [], []
        for r in range(size):
            inner = dot(mid_blocks[r], up_full, 1, 0) + up_shift.reshape(-1)
            value, pull = jax.vjp(lambda u: jax.nn.gelu(u, approximate=True), inner)
            active.append(value.astype(LOW))
            inner_grad.append(pull(dot(grad_blocks[r], down_full, 1, 1))[0].astype(LOW))
        mid_norm_grad = spread_blocks(lambda r: dot(inner_grad[r], up_full, 1, 1), size)
        middle_back, gain_mid, shift_mid = jax.vjp(
            norm_rows, middle, gain_rows[1], shift_rows[1]
        )[1](mid_norm_grad)
        middle_grad = out_grad.astype(F32) + middle_back
        middle_low = middle_grad.astype(LOW)
        middle_blocks = gather_blocks(middle_low, size)

        branch = spread_blocks(lambda r: dot(active[r], down_full, 1, 0), size)
        output = (middle + branch + down_shift).astype(LOW)

        active = jnp.concatenate(active)
        inner_grad = jnp.concatenate(inner_grad)
        up_grad = dot(jnp.concatenate(mid_blocks), inner_grad, 0, 0).astype(LOW)
        down_grad = dot(active, jnp.concatenate(grad_blocks), 0, 0).astype(LOW)
        up_sum = lax.psum_scatter(up_grad, "dp", scatter_dimension=0, tiled=True).astype(F32)
        down_sum = lax.psum_scatter(down_grad, "dp", scatter_dimension=1, tiled=True).astype(F32)
        up_shift_grad = jnp.sum(inner_grad, axis=0, dtype=F32).reshape(up_bias.shape[0], -1)
        down_shift_grad = jnp.sum(out_grad, axis=0, dtype=F32)

        middle_all = jnp.concatenate(middle_blocks)
        heads_grad = jnp.concatenate(
            [dot(b, out_full, 1, 1).astype(LOW) for b in middle_blocks]
        )
        out_shift_grad = jnp.sum(middle_low, axis=0, dtype=F32)
        out_weight_grad = dot(heads, middle_all, 0, 0).astype(LOW)
        out_weight_sum = lax.psum_scatter(
            out_weight_grad, "dp", scatter_dimension=1, tiled=True
        ).astype(F32)
        mixed_grads = attend_backward(plan, query, keys, values, heads, heads_grad, lse)
        flat_grad = jnp.concatenate(mixed_grads, axis=1)
        normed_terms = [dot(block_of(flat_grad, r), qkv_full, 1, 1) for r in range(size)]
        normed_grad = spread_blocks(lambda r: normed_terms[r], size)
        qkv_grad = dot(normed, flat_grad, 0, 0).astype(LOW)
        qkv_sum = lax.psum_scatter(qkv_grad, "dp", scatter_dimension=0, tiled=True)
        qkv_sum = qkv_sum.astype(F32).reshape(part, 3, local_width)
        query_sum = jnp.sum(mixed_grads[0], axis=0, dtype=F32).reshape(local_heads, HD)
        value_sum = jnp.sum(mixed_grads[2], axis=0, dtype=F32).reshape(local_heads, HD)
        qv_grad = jnp.concatenate([query_sum, value_sum], axis=1)

        gain_first = sum(
            jnp.sum(term * standard_rows(b.astype(F32)), axis=0)
            for term, b in zip(normed_terms, token_blocks)
        )
        shift_first = sum(jnp.sum(term, axis=0) for term in normed_terms)
        input_back = jax.vjp(lambda v: norm_rows(v, gain_rows[0], shift_rows[0]), inputs)[1](
            normed_grad
        )[0]
        input_grad = middle_grad + input_back

        both = jnp.stack(
            [gain_first, gain_mid, shift_first, shift_mid, out_shift_grad, down_shift_grad]
        )
        both = both.reshape(6, dp_size, part).transpose(1, 0, 2).reshape(dp_size, -1)
        single = [
            g.reshape(g.shape[0], dp_size, -1).transpose(1, 0, 2).reshape(dp_size, -1)
            for g in (qv_grad, up_shift_grad)
        ]
        sums = jnp.concatenate([both] + single, axis=1)
        span = sums.shape[1]
        padded = -(-span // 1024) * 1024
        sums = jnp.pad(sums, ((0, 0), (0, padded - span))).reshape(dp_size * padded // 128, 128)
        sums = lax.psum_scatter(sums, "dp", scatter_dimension=0, tiled=True).reshape(-1)
        across = lax.psum(sums[: 6 * part].reshape(6, part), "tensor")
        qv_sum = sums[6 * part : 6 * part + qv_bias.size].reshape(qv_bias.shape)
        up_shift_sum = sums[6 * part + qv_bias.size : span].reshape(up_bias.shape)
        return (
            output,
            input_grad,
            across[0:2],
            across[2:4],
            qkv_sum,
            qv_sum,
            out_weight_sum,
            across[4],
            up_sum,
            up_shift_sum,
            down_sum,
            across[5],
        )

    return run


def solution(mesh):
    placed = (
        P(("dp", "tensor"), None),
        P("dp"),
        P(None, "dp"),
        P(None, "dp"),
        P("dp", None, "tensor"),
        P("tensor", "dp"),
        P("tensor", "dp"),
        P("dp"),
        P("dp", "tensor"),
        P("tensor", "dp"),
        P("tensor", "dp"),
        P("dp"),
        P(("dp", "tensor"), None),
    )
    return jax.shard_map(
        on_device(mesh.shape["tensor"], mesh.shape["dp"]),
        mesh=mesh,
        in_specs=placed,
        out_specs=(
            P(("dp", "tensor"), None),
            P(("dp", "tensor"), None),
            P(None, "dp"),
            P(None, "dp"),
            P("dp", None, "tensor"),
            P("tensor", "dp"),
            P("tensor", "dp"),
            P("dp"),
            P("dp", "tensor"),
            P("tensor", "dp"),
            P("tensor", "dp"),
            P("dp"),
        ),
        check_vma=False,
    )
```

time: 1480 us -> 535 us (0.36)
  waiting for transfers between devices: 788 us -> 180 us
  matrix products: 298 us -> 108 us
  blocking collectives: 174 us -> 71.1 us
  other arithmetic: 118 us -> 34.8 us
  Pallas kernels: 0 us -> 69.6 us
  local copies, waits for them, and re-layouts: 64.8 us -> 29.5 us
    reduce_scatter x8 -> x2, waiting for transfers between devices: 447 us -> 13.4 us  [the longest x1 13.4 us: run(): qkv_sum = lax.psum_scatter(qkv_grad, 'dp', scatter_dimension=0, tiled=True)]
    dot_general x40 -> x33, matrix products: 298 us -> 108 us  [dot(): lax.dot_general(left, right, (((left_dim,), (right_dim,)), ((), ())), pre...]
    all_gather x7 -> x3, waiting for transfers between devices: 166 us -> 10.9 us  [the longest x1 10.9 us: run(): packed = lax.all_gather(packed, 'dp', axis=0)]
    unnamed x23 -> x9, waiting for transfers between devices: 176 us -> 54.6 us
    all_gather x7 -> x1, blocking collectives: 148 us -> 30.2 us  [run(): out_full = lax.all_gather(out_weight, 'dp', axis=1, tiled=True)]
    ppermute x0 -> x24, waiting for transfers between devices: none -> 101 us  [swap(): lax.ppermute(value, 'tensor', [(place, place ^ bit) for place in range(si...]
    pallas_call x0 -> x2, Pallas kernels: none -> 69.6 us  [the longest x1 34.9 us: attend_forward(): pl.pallas_call(forward_kernel, grid=(count,), out_shape=(jax.ShapeDtypeSt...]
    convert_element_type x19 -> x8, other arithmetic: 55.8 us -> 7.06 us  [the longest x1 3.27 us: run(): norm_rows(b.astype(F32), gain_rows[0], shift_rows[0]).astype(LOW)]
  transfers between devices with their start and end apart: 19 -> 31, of which waited for: 17 -> 9; matrix products, arithmetic and copies ran while one was open for 7% -> 26% of each run, Pallas kernels for 0% -> 13%
where the time goes in v1:
time: 535 us; the launch traced here: 525 us
  waiting for transfers between devices  180 us (34%)
  matrix products  108 us (20%)
  blocking collectives  71.1 us (13%)
  Pallas kernels  69.6 us (13%)
  other arithmetic  34.8 us (7%)
  local copies, waits for them, and re-layouts  29.5 us (6%)
  between operations  16.2 us (3%)
  starting transfers between devices  15.2 us (3%)
    dot_general x33, matrix products, dot(): lax.dot_general(left, right, (((left_dim,), (right_dim,)), ((), ())), pre...  108 us
    ppermute x24, waiting for transfers between devices, swap(): lax.ppermute(value, 'tensor', [(place, place ^ bit) for place in range(si...  101 us
    unnamed x9, waiting for transfers between devices  54.6 us
    unnamed x1, blocking collectives  35.3 us
    pallas_call x1, Pallas kernels, attend_forward(): pl.pallas_call(forward_kernel, grid=(count,), out_shape=(jax.ShapeDtypeSt...  34.9 us
    pallas_call x1, Pallas kernels, attend_backward(): pl.pallas_call(backward_kernel, grid=(count,), out_shape=(jax.ShapeDtypeS...  34.7 us
    all_gather x1, blocking collectives, run(): out_full = lax.all_gather(out_weight, 'dp', axis=1, tiled=True)  30.2 us
    unnamed x129, local copies, waits for them, and re-layouts  17.3 us
  transfers between devices with their start and end apart: 31, of which 9 were waited for; matrix products, arithmetic and copies ran while one was open for 26% of the time, Pallas kernels for 13%

profile of v1, /device:TPU:0, one launch (start us, length us, event | category | flops | bytes accessed | tf_op | source)
XLA Modules:
  0.0 525.1 jit_solution(4796289425555400920)
XLA Ops:
  13.9 3.0 collective-permute-start.1
  18.9 30.2 %all_gather.17 = bf16[256,1024]{1,0:T(8,128)(2,1)S(1)} all-gather(bf16[256,128]{1,0:T(8,128)(2,1)S(1)} %copy-done.36), channel_id=1, replica_groups=mesh['dp'=8,'tensor'=4] {'dp'}, dimensions={1}, use_global_device_ids=true | all-gather | bytes 589824 | tf_op jit(solution)/shard_map/all_gather | solution.py:305
  54.6 10.9 %all-gather.9.cloned.1.call-done = bf16[1152,768]{1,0:T(8,128)(2,1)} async-done(((bf16[144,768]{1,0:T(8,128)(2,1)}), bf16[1152,768]{1,0:T(8,128)(2,1)}) %all-gather.9.cloned.1.call-update) | async-done | bytes 1769488 | tf_op jit(solution)/shard_map/all_gather | solution.py:292
  68.6 3.3 fusion.50
  72.0 7.2 %add_convert_fusion = bf16[2048,768]{1,0:T(8,128)(2,1)S(1)} fusion(bf16[1024,768]{1,0:T(8,128)(2,1)S(1)} %bitcast.134, f32[768]{0:T(1024)S(1)} %pad_maximum_fusion.7, bf16[512,1024]{1,0:T(8,128)(2,1)S(1)} %get-tuple-element.122, bf16[512,1024]{1,0:T(8,128)(2,1)S(1)} %get-tuple-element.121, bf16[512,1024]{1,0:T(8,128)(2,1)S(1)} %get-tuple-element.120, ...), kind=kOutput, calls=%fused_computation.1 | convolution fusion | flops 3241148416 | bytes 8915968 | tf_op jit(solution)/shard_map/dot_general | solution.py:33
  79.5 34.9 %attend_forward.1 = (bf16[2048,256]{1,0:T(8,128)(2,1)S(1)}, f32[8,4,256]{2,1,0:T(4,128)S(1)}) custom-call(s32[8]{0:T(128)S(1)} %get-tuple-element.92.first_ref, s32[8]{0:T(128)S(1)} %get-tuple-element.91.clear_ref, s32[8]{0:T(128)S(1)} %get-tuple-element.138.phys_ref, f32[4]{0:T(128)S(1)} %power_multiply_fusion.slope_ref, ...), custom_call_target="tpu_custom_call" | custom-call | flops 2147483648 | bytes 4194304 | tf_op jit(solution)/shard_map/attend_forward/pallas_call | solution.py:213
  124.2 17.9 %collective-permute-done.14 = bf16[512,1024]{1,0:T(8,128)(2,1)} collective-permute-done((bf16[512,1024]{1,0:T(8,128)(2,1)}, bf16[512,1024]{1,0:T(8,128)(2,1)}, u32[]{:S(2)}, u32[]{:S(2)}) %collective-permute-start.14) | collective-permute-done | bytes 1048608 | tf_op jit(solution)/shard_map/ppermute | solution.py:39
  144.2 4.8 fusion.153
  149.0 15.3 %collective-permute-done.5 = bf16[512,1024]{1,0:T(8,128)(2,1)} collective-permute-done((bf16[512,1024]{1,0:T(8,128)(2,1)}, bf16[512,1024]{1,0:T(8,128)(2,1)}, u32[]{:S(2)}, u32[]{:S(2)}) %collective-permute-start.5) | collective-permute-done | bytes 1048608 | tf_op jit(solution)/shard_map/ppermute | solution.py:39
  169.3 3.8 fusion.150
  173.1 3.9 fusion.154
  177.0 3.9 fusion.152
  180.9 11.7 %collective-permute-done.8 = bf16[512,1024]{1,0:T(8,128)(2,1)} collective-permute-done((bf16[512,1024]{1,0:T(8,128)(2,1)S(1)}, bf16[512,1024]{1,0:T(8,128)(2,1)}, u32[]{:S(2)}, u32[]{:S(2)}) %collective-permute-start.8) | collective-permute-done | bytes 1048608 | tf_op jit(solution)/shard_map/ppermute | solution.py:39
  201.6 9.7 %fusion.77 = (bf16[512,1024]{1,0:T(8,128)(2,1)S(1)}, bf16[512,1024]{1,0:T(8,128)(2,1)S(1)}, bf16[512,1024]{1,0:T(8,128)(2,1)S(1)}, bf16[512,1024]{1,0:T(8,128)(2...) fusion(f32[512,1024]{1,0:T(8,128)S(1)} %copy-done.50, ...), kind=kOutput, calls=%fused_computation.102 | convolution fusion | flops 1121976320 | bytes 26218496 | tf_op jit(solution)/shard_map/dot_general | solution.py:33
  213.3 8.3 %fusion.95 = bf16[1024,1024]{1,0:T(8,128)(2,1)} fusion(bf16[512,1024]{1,0:T(8,128)(2,1)} %collective-permute-done.15, bf16[512,1024]{1,0:T(8,128)(2,1)} %collective-permute-done.14, bf16[512,1024]{1,0:T(8,128)(2,1)} %collective-permute-done.12, bf16[512,1024]{1,0:T(8,128)(2,1)} %param.25, bf16[512,1024]{1,0:T(8,128)(2,1)S(1)} %get-tuple-element.129, ...), kind=kOutput, calls=%fused_computation.139 | convolution fusion | flops 4329570304 | bytes 10485760 | tf_op jit(solution)/shard_map/dot_general | solution.py:33
  221.7 3.9 copy.49
  225.9 3.3 convolution_convert_fusion.1
  241.8 20.0 %collective-permute-done.17 = bf16[512,1024]{1,0:T(8,128)(2,1)S(1)} collective-permute-done((bf16[512,1024]{1,0:T(8,128)(2,1)S(1)}, bf16[512,1024]{1,0:T(8,128)(2,1)S(1)}, u32[]{:S(2)}, u32[]{:S(2)}) %collective-permute-start.17) | collective-permute-done | bytes 1048608 | tf_op jit(solution)/shard_map/ppermute | solution.py:39
  262.8 20.9 %collective-permute-done.11 = bf16[512,1024]{1,0:T(8,128)(2,1)S(1)} collective-permute-done((bf16[512,1024]{1,0:T(8,128)(2,1)S(1)}, bf16[512,1024]{1,0:T(8,128)(2,1)S(1)}, u32[]{:S(2)}, u32[]{:S(2)}) %collective-permute-start.11) | collective-permute-done | bytes 1048608 | tf_op jit(solution)/shard_map/ppermute | solution.py:39
  285.8 3.4 convert_reduce_fusion.8
  290.7 8.1 %fusion.100 = bf16[1024,1024]{1,0:T(8,128)(2,1)} fusion(bf16[512,1024]{1,0:T(8,128)(2,1)} %collective-permute-done.9, bf16[512,1024]{1,0:T(8,128)(2,1)} %collective-permute-done.8, bf16[512,1024]{1,0:T(8,128)(2,1)} %collective-permute-done.6, bf16[512,1024]{1,0:T(8,128)(2,1)S(1)} %copy-done.32, bf16[512,1024]{1,0:T(8,128)(2,1)S(1)} %copy-done.29, ...), kind=kOutput, calls=%fused_computation.140 | convolution fusion | flops 4329570304 | bytes 10485760 | tf_op jit(solution)/shard_map/dot_general | solution.py:33
  298.7 15.6 %collective-permute-done.19 = bf16[512,1024]{1,0:T(8,128)(2,1)} collective-permute-done((bf16[512,1024]{1,0:T(8,128)(2,1)}, bf16[512,1024]{1,0:T(8,128)(2,1)}, u32[]{:S(2)}, u32[]{:S(2)}) %collective-permute-start.19) | collective-permute-done | bytes 1048608 | tf_op jit(solution)/shard_map/ppermute | solution.py:39
  324.1 3.4 fusion.104
  331.4 34.7 %attend_backward.1 = (bf16[2048,256]{1,0:T(8,128)(2,1)S(1)}, bf16[2048,256]{1,0:T(8,128)(2,1)S(1)}, bf16[2048,256]{1,0:T(8,128)(2,1)S(1)}) custom-call(s32[8]{0:T(128)S(1)} %get-tuple-element.92.first_ref, s32[8]{0:T(128)S(1)} %get-tuple-element.91.clear_ref, s32[8]{0:T(128)S(1)} %get-tuple-element.138.phys_ref, f32[4]{0:T(128)S(1)} %power_multiply_fusion.slope_ref, ...), custom_call_target="tpu_custom_call" | custom-call | flops 5368709120 | bytes 8388608 | tf_op jit(solution)/shard_map/attend_backward/pallas_call | solution.py:237
  370.5 3.3 fusion.135
  382.2 7.4 %convolution_convert_fusion = bf16[1024,768]{1,0:T(8,128)(2,1)} fusion(bf16[2048,768]{1,0:T(8,128)(2,1)} %copy-done.33, bf16[512,1024]{1,0:T(8,128)(2,1)} %copy-done.27, bf16[512,1024]{1,0:T(8,128)(2,1)} %copy-done.26, bf16[512,1024]{1,0:T(8,128)(2,1)S(1)} %copy-done.25, bf16[512,1024]{1,0:T(8,128)(2,1)S(1)} %copy-done.23), kind=kOutput, calls=%fused_computation.141 | convolution fusion | flops 3238789120 | bytes 8912896 | tf_op jit(solution)/shard_map/dot_general | solution.py:33
  393.5 54.4 %reduce-scatter.13.cloned.1.call-done = bf16[128,256]{1,0:T(8,128)(2,1)} async-done(((bf16[1024,256]{1,0:T(8,128)(2,1)}), bf16[128,256]{1,0:T(8,128)(2,1)}) %reduce-scatter.13.cloned.1.call-update) | async-done | bytes 65552
  449.6 3.5 fusion.51
  455.9 3.1 convert_reduce_fusion.2
  459.1 35.3 %all-reduce.2 = f32[64,128]{1,0:T(8,128)S(1)} all-reduce(f32[64,128]{1,0:T(8,128)S(1)} %reshape.396), channel_id=3, replica_groups=mesh['dp'=8,'tensor'=4] {'dp'}, use_global_device_ids=true, to_apply=%region_31.32.clone | all-reduce | flops 8192 | bytes 65536
  495.7 5.6 %psum.7 = f32[6,128]{1,0:T(8,128)S(1)} all-reduce(f32[6,128]{1,0:T(8,128)S(1)} %bitcast.150), channel_id=1, replica_groups=mesh['dp'=8,'tensor'=4] {'tensor'}, use_global_device_ids=true, to_apply=%region_32.33 | all-reduce | flops 768 | bytes 6144 | tf_op jit(solution)/shard_map/psum | solution.py:404
  502.4 13.4 %reduce-scatter.9.cloned.1.call-done = bf16[128,768]{1,0:T(8,128)(2,1)} async-done(((bf16[1024,768]{1,0:T(8,128)(2,1)}), bf16[128,768]{1,0:T(8,128)(2,1)}) %reduce-scatter.9.cloned.1.call-update) | async-done | bytes 196624 | tf_op jit(solution)/shard_map/reduce_scatter | solution.py:375
  (303 shorter events, 100.5 us)
Async XLA Ops:
  7.2 58.3 %all-gather.9.cloned.1.call-start = ((), (), s32[]{:S(2)}) async-start(), calls=%async_computation.8 | async-start | bytes 1990656 | tf_op jit(solution)/shard_map/all_gather | solution.py:292
  13.9 130.3 %all-gather.7.cloned.1.call-start = ((), (), s32[]{:S(2)}) async-start(), calls=%async_computation.5 | async-start | bytes 2359296 | tf_op jit(solution)/shard_map/all_gather | solution.py:307
  13.9 35.1 %collective-permute-start.1 = (bf16[512,1024]{1,0:T(8,128)(2,1)S(1)}, bf16[512,1024]{1,0:T(8,128)(2,1)S(1)}, u32[]{:S(2)}, u32[]{:S(2)}) collective-permute-start(bf16[512,1024]{1,0:T(8,128)(2,1)S(1)} %copy-done.6), channel_id=1, source_target_pairs={{0,2},{1,3},{2,0},{3,1},{4,6},{5,7},{6,4},{7,5},{8,10},{9,11},{10,... | collective-permute-start | bytes 3145736 | tf_op jit(solution)/shard_map/ppermute | solution.py:39
  17.0 32.4 %collective-permute-start = (bf16[512,1024]{1,0:T(8,128)(2,1)S(1)}, bf16[512,1024]{1,0:T(8,128)(2,1)}, u32[]{:S(2)}, u32[]{:S(2)}) collective-permute-start(bf16[512,1024]{1,0:T(8,128)(2,1)S(1)} %copy-done.6), channel_id=1, source_target_pairs={{0,1},{1,0},{2,3},{3,2},{4,5},{5,4},{6,7},{7,6},{8,9},{9,8},{10,11... | collective-permute-start | bytes 3145736 | tf_op jit(solution)/shard_map/ppermute | solution.py:39
  17.0 175.7 %all-gather.5.cloned.1.call-start = ((), (), s32[]{:S(2)}) async-start(), calls=%async_computation.4 | async-start | bytes 2359296 | tf_op jit(solution)/shard_map/all_gather | solution.py:306
  49.1 4.1 collective-permute-start.2
  114.4 209.6 %copy-start.3 = (bf16[2048,256]{1,0:T(8,128)(2,1)}, bf16[2048,256]{1,0:T(8,128)(2,1)S(1)}, u32[]{:S(2)}) copy-start(bf16[2048,256]{1,0:T(8,128)(2,1)S(1)} %get-tuple-element.17.out_ref) | copy-start | bytes 3145732
  115.9 3.6 collective-permute-start.4
  115.9 26.3 %collective-permute-start.14 = (bf16[512,1024]{1,0:T(8,128)(2,1)}, bf16[512,1024]{1,0:T(8,128)(2,1)}, u32[]{:S(2)}, u32[]{:S(2)}) collective-permute-start(bf16[512,1024]{1,0:T(8,128)(2,1)} %param.25), channel_id=1, source_target_pairs={{0,2},{1,3},{2,0},{3,1},{4,6},{5,7},{6,4},{7,5},{8,10},{9,11},{10,... | collective-permute-start | bytes 3145736 | tf_op jit(solution)/shard_map/ppermute | solution.py:39
  117.4 272.2 %reduce-scatter.15.cloned.1.call-start = ((), (), s32[]{:S(2)}) async-start(), calls=%async_computation.10 | async-start | bytes 2359296
  119.2 29.8 %collective-permute-start.3 = (bf16[512,1024]{1,0:T(8,128)(2,1)}, bf16[512,1024]{1,0:T(8,128)(2,1)}, u32[]{:S(2)}, u32[]{:S(2)}) collective-permute-start(bf16[512,1024]{1,0:T(8,128)(2,1)} %convolution_convert_fusion.6), channel_id=1, source_target_pairs={{0,1},{1,0},{2,3},{3,2},{4,5},{5,4},{6,7},{7,6},{8,9},{9,8},{10,11... | collective-permute-start | bytes 3145736 | tf_op jit(solution)/shard_map/ppermute | solution.py:39
  122.1 42.2 %collective-permute-start.5 = (bf16[512,1024]{1,0:T(8,128)(2,1)}, bf16[512,1024]{1,0:T(8,128)(2,1)}, u32[]{:S(2)}, u32[]{:S(2)}) collective-permute-start(bf16[512,1024]{1,0:T(8,128)(2,1)} %add_convert_fusion.6), channel_id=1, source_target_pairs={{0,2},{1,3},{2,0},{3,1},{4,6},{5,7},{6,4},{7,5},{8,10},{9,11},{10,... | collective-permute-start | bytes 3145736 | tf_op jit(solution)/shard_map/ppermute | solution.py:39
  123.0 54.0 %collective-permute-start.12 = (bf16[512,1024]{1,0:T(8,128)(2,1)}, bf16[512,1024]{1,0:T(8,128)(2,1)}, u32[]{:S(2)}, u32[]{:S(2)}) collective-permute-start(bf16[512,1024]{1,0:T(8,128)(2,1)} %param.25), channel_id=1, source_target_pairs={{0,1},{1,0},{2,3},{3,2},{4,5},{5,4},{6,7},{7,6},{8,9},{9,8},{10,11... | collective-permute-start | bytes 3145736 | tf_op jit(solution)/shard_map/ppermute | solution.py:39
  142.1 30.9 %collective-permute-start.15 = (bf16[512,1024]{1,0:T(8,128)(2,1)}, bf16[512,1024]{1,0:T(8,128)(2,1)}, u32[]{:S(2)}, u32[]{:S(2)}) collective-permute-start(bf16[512,1024]{1,0:T(8,128)(2,1)} %collective-permute-done.14), channel_id=1, source_target_pairs={{0,1},{1,0},{2,3},{3,2},{4,5},{5,4},{6,7},{7,6},{8,9},{9,8},{10,11... | collective-permute-start | bytes 3145736 | tf_op jit(solution)/shard_map/ppermute | solution.py:39
  167.8 24.9 %collective-permute-start.8 = (bf16[512,1024]{1,0:T(8,128)(2,1)S(1)}, bf16[512,1024]{1,0:T(8,128)(2,1)}, u32[]{:S(2)}, u32[]{:S(2)}) collective-permute-start(bf16[512,1024]{1,0:T(8,128)(2,1)S(1)} %add_convert_fusion.5), channel_id=1, source_target_pairs={{0,2},{1,3},{2,0},{3,1},{4,6},{5,7},{6,4},{7,5},{8,10},{9,11},{10,... | collective-permute-start | bytes 3145736 | tf_op jit(solution)/shard_map/ppermute | solution.py:39
  177.0 21.4 %collective-permute-start.6 = (bf16[512,1024]{1,0:T(8,128)(2,1)S(1)}, bf16[512,1024]{1,0:T(8,128)(2,1)}, u32[]{:S(2)}, u32[]{:S(2)}) collective-permute-start(bf16[512,1024]{1,0:T(8,128)(2,1)S(1)} %add_convert_fusion.5), channel_id=1, source_target_pairs={{0,1},{1,0},{2,3},{3,2},{4,5},{5,4},{6,7},{7,6},{8,9},{9,8},{10,11... | collective-permute-start | bytes 3145736 | tf_op jit(solution)/shard_map/ppermute | solution.py:39
  192.7 8.4 %collective-permute-start.9 = (bf16[512,1024]{1,0:T(8,128)(2,1)}, bf16[512,1024]{1,0:T(8,128)(2,1)}, u32[]{:S(2)}, u32[]{:S(2)}) collective-permute-start(bf16[512,1024]{1,0:T(8,128)(2,1)} %collective-permute-done.8), channel_id=1, source_target_pairs={{0,1},{1,0},{2,3},{3,2},{4,5},{5,4},{6,7},{7,6},{8,9},{9,8},{10,11... | collective-permute-start | bytes 3145736 | tf_op jit(solution)/shard_map/ppermute | solution.py:39
  225.6 166.1 %reduce-scatter.11.cloned.1.call-start = ((), (), s32[]{:S(2)}) async-start(), calls=%async_computation.7 | async-start | bytes 2359296 | tf_op jit(solution)/shard_map/reduce_scatter | solution.py:356
  229.2 5.1 collective-permute-start.16
  231.1 6.2 %collective-permute-start.10 = (bf16[512,1024]{1,0:T(8,128)(2,1)S(1)}, bf16[512,1024]{1,0:T(8,128)(2,1)S(1)}, u32[]{:S(2)}, u32[]{:S(2)}) collective-permute-start(bf16[512,1024]{1,0:T(8,128)(2,1)S(1)} %convolution_convert_fusion.3), channel_id=1, source_target_pairs={{0,1},{1,0},{2,3},{3,2},{4,5},{5,4},{6,7},{7,6},{8,9},{9,8},{10,11... | collective-permute-start | bytes 3145736 | tf_op jit(solution)/shard_map/ppermute | solution.py:39
  232.5 9.3 %collective-permute-start.13 = (bf16[512,1024]{1,0:T(8,128)(2,1)S(1)}, bf16[512,1024]{1,0:T(8,128)(2,1)S(1)}, u32[]{:S(2)}, u32[]{:S(2)}) collective-permute-start(bf16[512,1024]{1,0:T(8,128)(2,1)S(1)} %convolution_convert_fusion.2), channel_id=1, source_target_pairs={{0,1},{1,0},{2,3},{3,2},{4,5},{5,4},{6,7},{7,6},{8,9},{9,8},{10,11... | collective-permute-start | bytes 3145736 | tf_op jit(solution)/shard_map/ppermute | solution.py:39
  234.3 28.5 %collective-permute-start.7 = (bf16[512,1024]{1,0:T(8,128)(2,1)S(1)}, bf16[512,1024]{1,0:T(8,128)(2,1)S(1)}, u32[]{:S(2)}, u32[]{:S(2)}) collective-permute-start(bf16[512,1024]{1,0:T(8,128)(2,1)S(1)} %convolution_convert_fusion.4), channel_id=1, source_target_pairs={{0,1},{1,0},{2,3},{3,2},{4,5},{5,4},{6,7},{7,6},{8,9},{9,8},{10,11... | collective-permute-start | bytes 3145736 | tf_op jit(solution)/shard_map/ppermute | solution.py:39
  235.7 26.0 %collective-permute-start.17 = (bf16[512,1024]{1,0:T(8,128)(2,1)S(1)}, bf16[512,1024]{1,0:T(8,128)(2,1)S(1)}, u32[]{:S(2)}, u32[]{:S(2)}) collective-permute-start(bf16[512,1024]{1,0:T(8,128)(2,1)S(1)} %add_convert_fusion.2), channel_id=1, source_target_pairs={{0,2},{1,3},{2,0},{3,1},{4,6},{5,7},{6,4},{7,5},{8,10},{9,11},{10,... | collective-permute-start | bytes 3145736 | tf_op jit(solution)/shard_map/ppermute | solution.py:39
  238.5 45.2 %collective-permute-start.11 = (bf16[512,1024]{1,0:T(8,128)(2,1)S(1)}, bf16[512,1024]{1,0:T(8,128)(2,1)S(1)}, u32[]{:S(2)}, u32[]{:S(2)}) collective-permute-start(bf16[512,1024]{1,0:T(8,128)(2,1)S(1)} %add_convert_fusion.4), channel_id=1, source_target_pairs={{0,2},{1,3},{2,0},{3,1},{4,6},{5,7},{6,4},{7,5},{8,10},{9,11},{10,... | collective-permute-start | bytes 3145736 | tf_op jit(solution)/shard_map/ppermute | solution.py:39
  289.2 25.2 %collective-permute-start.19 = (bf16[512,1024]{1,0:T(8,128)(2,1)}, bf16[512,1024]{1,0:T(8,128)(2,1)}, u32[]{:S(2)}, u32[]{:S(2)}) collective-permute-start(bf16[512,1024]{1,0:T(8,128)(2,1)} %get-tuple-element.83), channel_id=1, source_target_pairs={{0,2},{1,3},{2,0},{3,1},{4,6},{5,7},{6,4},{7,5},{8,10},{9,11},{10,... | collective-permute-start | bytes 3145736 | tf_op jit(solution)/shard_map/ppermute | solution.py:39
  290.6 31.0 %collective-permute-start.18 = (bf16[512,1024]{1,0:T(8,128)(2,1)}, bf16[512,1024]{1,0:T(8,128)(2,1)}, u32[]{:S(2)}, u32[]{:S(2)}) collective-permute-start(bf16[512,1024]{1,0:T(8,128)(2,1)} %get-tuple-element.83), channel_id=1, source_target_pairs={{0,1},{1,0},{2,3},{3,2},{4,5},{5,4},{6,7},{7,6},{8,9},{9,8},{10,11... | collective-permute-start | bytes 3145736 | tf_op jit(solution)/shard_map/ppermute | solution.py:39
  314.3 9.7 %collective-permute-start.20 = (bf16[512,1024]{1,0:T(8,128)(2,1)}, bf16[512,1024]{1,0:T(8,128)(2,1)}, u32[]{:S(2)}, u32[]{:S(2)}) collective-permute-start(bf16[512,1024]{1,0:T(8,128)(2,1)} %collective-permute-done.19), channel_id=1, source_target_pairs={{0,1},{1,0},{2,3},{3,2},{4,5},{5,4},{6,7},{7,6},{8,9},{9,8},{10,11... | collective-permute-start | bytes 3145736 | tf_op jit(solution)/shard_map/ppermute | solution.py:39
  316.7 131.2 %reduce-scatter.13.cloned.1.call-start = ((), (), s32[]{:S(2)}) async-start(), calls=%async_computation.9 | async-start | bytes 589824
  370.0 7.6 %collective-permute-start.22 = (bf16[512,1024]{1,0:T(8,128)(2,1)}, bf16[512,1024]{1,0:T(8,128)(2,1)}, u32[]{:S(2)}, u32[]{:S(2)}) collective-permute-start(bf16[512,1024]{1,0:T(8,128)(2,1)} %get-tuple-element.106), channel_id=1, source_target_pairs={{0,1},{1,0},{2,3},{3,2},{4,5},{5,4},{6,7},{7,6},{8,9},{9,8},{10,11... | collective-permute-start | bytes 3145736 | tf_op jit(solution)/shard_map/ppermute | solution.py:39
  373.8 75.8 %collective-permute-start.21 = (bf16[512,1024]{1,0:T(8,128)(2,1)}, bf16[512,1024]{1,0:T(8,128)(2,1)}, u32[]{:S(2)}, u32[]{:S(2)}) collective-permute-start(bf16[512,1024]{1,0:T(8,128)(2,1)} %get-tuple-element.104), channel_id=1, source_target_pairs={{0,1},{1,0},{2,3},{3,2},{4,5},{5,4},{6,7},{7,6},{8,9},{9,8},{10,11... | collective-permute-start | bytes 3145736 | tf_op jit(solution)/shard_map/ppermute | solution.py:39
  374.6 141.2 %reduce-scatter.9.cloned.1.call-start = ((), (), s32[]{:S(2)}) async-start(), calls=%async_computation.6 | async-start | bytes 1769472 | tf_op jit(solution)/shard_map/reduce_scatter | solution.py:375
  380.6 69.0 %collective-permute-start.23 = (bf16[512,1024]{1,0:T(8,128)(2,1)}, bf16[512,1024]{1,0:T(8,128)(2,1)}, u32[]{:S(2)}, u32[]{:S(2)}) collective-permute-start(bf16[512,1024]{1,0:T(8,128)(2,1)} %get-tuple-element.105), channel_id=1, source_target_pairs={{0,2},{1,3},{2,0},{3,1},{4,6},{5,7},{6,4},{7,5},{8,10},{9,11},{10,... | collective-permute-start | bytes 3145736 | tf_op jit(solution)/shard_map/ppermute | solution.py:39
  (56 other events, 582.6 us)
Sparse Core Ops, SparseCore 0:
  14.0 51.4 all-gather.8
  67.5 50.0 all-gather.6
  119.7 47.6 all-gather.4
  225.8 66.7 reduce-scatter.14
  316.8 66.9 reduce-scatter.10
  387.0 60.8 reduce-scatter.12
  451.8 63.9 reduce-scatter.8

commit v2 on v1

--- a/solution.py
+++ b/solution.py
@@ -50,17 +50,25 @@
     return blocks
 
 
-def spread_blocks(term, size):
+def spread_blocks(term, size, later=None):
+    if later is not None:
+        if size == 4:
+            across, later = lax.optimization_barrier((swap(term(3).astype(LOW), 1, size), later))
+            return spread_after(term, size, across), later
+        return spread_blocks(term, size), later
     if size == 4:
-        across = swap(term(3).astype(LOW), 1, size)
-        partner = term(2) + across.astype(F32)
-        partner = swap(partner.astype(LOW), 2, size)
-        beside = swap(term(1).astype(LOW), 1, size)
-        return term(0) + beside.astype(F32) + partner.astype(F32)
+        return spread_after(term, size, swap(term(3).astype(LOW), 1, size))
     total = term(0)
     for bit in range(1, size):
         total = total + swap(term(bit).astype(LOW), bit, size).astype(F32)
     return total
+
+
+def spread_after(term, size, across):
+    partner = term(2) + across.astype(F32)
+    partner = swap(partner.astype(LOW), 2, size)
+    beside = swap(term(1).astype(LOW), 1, size)
+    return term(0) + beside.astype(F32) + partner.astype(F32)
 
 
 def column_of(index):
@@ -286,11 +294,15 @@
         pieces = [norm_gains.reshape(-1), norm_biases.reshape(-1), out_bias, down_bias,
                   qv_bias.reshape(-1), up_bias.reshape(-1)]
         small = jnp.concatenate(pieces)
-        extra = -(-small.shape[0] // (16 * width)) * 16
-        small = jnp.pad(small, (0, extra * width - small.shape[0])).reshape(extra, width)
-        packed = jnp.concatenate([qkv_weight.reshape(part, width), small], axis=0)
+        wide = width + local_width
+        extra = -(-small.shape[0] // (16 * wide)) * 16
+        small = jnp.pad(small, (0, extra * wide - small.shape[0])).reshape(extra, wide)
+        packed = jnp.concatenate([qkv_weight.reshape(part, width), out_weight.T], axis=1)
+        packed = jnp.concatenate([packed, small], axis=0)
         packed = lax.all_gather(packed, "dp", axis=0)
-        qkv_full = packed[:, :part].reshape(D, width)
+        attention_full = packed[:, :part].reshape(D, wide)
+        qkv_full = attention_full[:, :width]
+        out_full = attention_full[:, width:]
         small = packed[:, part:].reshape(dp_size, -1)
         full = []
         place = 0
@@ -302,9 +314,12 @@
             full.append(block.transpose(1, 0, 2).reshape(shape[0], -1).astype(F32))
             place += piece.size
         gain_rows, shift_rows, out_shift, down_shift, qv_full, up_shift = full
-        out_full = lax.all_gather(out_weight, "dp", axis=1, tiled=True)
-        up_full = lax.all_gather(up_weight, "dp", axis=0, tiled=True)
-        down_full = lax.all_gather(down_weight, "dp", axis=1, tiled=True)
+        units = up_weight.shape[1]
+        mlp_full = lax.all_gather(
+            jnp.concatenate([up_weight, down_weight.T], axis=1), "dp", axis=0, tiled=True
+        )
+        up_full = mlp_full[:, :units]
+        down_full = mlp_full[:, units:]
         grad_blocks = gather_blocks(out_grad, size)
 
         plan = attention_plan(segments, position, size, local_heads)
@@ -327,7 +342,9 @@
         def block_of(array, r):
             return array[r * rows : (r + 1) * rows]
 
-        projected = spread_blocks(lambda r: dot(block_of(heads, r), out_full, 1, 0), size)
+        projected = spread_blocks(lambda r: dot(block_of(heads, r), out_full, 1, 1), size)
+        active_grad = [dot(b, down_full, 1, 0) for b in grad_blocks]
+        projected, active_grad = lax.optimization_barrier((projected, active_grad))
         middle = inputs + projected + out_shift
         normed_mid = norm_rows(middle, gain_rows[1], shift_rows[1]).astype(LOW)
         mid_blocks = gather_blocks(normed_mid, size)
@@ -337,8 +354,10 @@
             inner = dot(mid_blocks[r], up_full, 1, 0) + up_shift.reshape(-1)
             value, pull = jax.vjp(lambda u: jax.nn.gelu(u, approximate=True), inner)
             active.append(value.astype(LOW))
-            inner_grad.append(pull(dot(grad_blocks[r], down_full, 1, 1))[0].astype(LOW))
-        mid_norm_grad = spread_blocks(lambda r: dot(inner_grad[r], up_full, 1, 1), size)
+            inner_grad.append(pull(active_grad[r])[0].astype(LOW))
+        mid_norm_grad, kept_grad = spread_blocks(
+            lambda r: dot(inner_grad[r], up_full, 1, 1), size, inner_grad
+        )
         middle_back, gain_mid, shift_mid = jax.vjp(
             norm_rows, middle, gain_rows[1], shift_rows[1]
         )[1](mid_norm_grad)
@@ -346,34 +365,40 @@
         middle_low = middle_grad.astype(LOW)
         middle_blocks = gather_blocks(middle_low, size)
 
-        branch = spread_blocks(lambda r: dot(active[r], down_full, 1, 0), size)
+        kept_active, heads, last = lax.optimization_barrier((active, heads, middle_blocks[-1]))
+        middle_blocks = middle_blocks[:-1] + [last]
+        branch = spread_blocks(lambda r: dot(kept_active[r], down_full, 1, 1), size)
         output = (middle + branch + down_shift).astype(LOW)
 
         active = jnp.concatenate(active)
-        inner_grad = jnp.concatenate(inner_grad)
+        inner_grad = jnp.concatenate(kept_grad)
         up_grad = dot(jnp.concatenate(mid_blocks), inner_grad, 0, 0).astype(LOW)
-        down_grad = dot(active, jnp.concatenate(grad_blocks), 0, 0).astype(LOW)
-        up_sum = lax.psum_scatter(up_grad, "dp", scatter_dimension=0, tiled=True).astype(F32)
-        down_sum = lax.psum_scatter(down_grad, "dp", scatter_dimension=1, tiled=True).astype(F32)
+        down_grad = dot(jnp.concatenate(grad_blocks), active, 0, 0).astype(LOW)
+        mlp_sum = lax.psum_scatter(
+            jnp.concatenate([up_grad, down_grad], axis=1), "dp", scatter_dimension=0, tiled=True
+        ).astype(F32)
+        up_sum = mlp_sum[:, :units]
+        down_sum = mlp_sum[:, units:].T
         up_shift_grad = jnp.sum(inner_grad, axis=0, dtype=F32).reshape(up_bias.shape[0], -1)
         down_shift_grad = jnp.sum(out_grad, axis=0, dtype=F32)
 
         middle_all = jnp.concatenate(middle_blocks)
         heads_grad = jnp.concatenate(
-            [dot(b, out_full, 1, 1).astype(LOW) for b in middle_blocks]
+            [dot(b, out_full, 1, 0).astype(LOW) for b in middle_blocks]
         )
         out_shift_grad = jnp.sum(middle_low, axis=0, dtype=F32)
-        out_weight_grad = dot(heads, middle_all, 0, 0).astype(LOW)
-        out_weight_sum = lax.psum_scatter(
-            out_weight_grad, "dp", scatter_dimension=1, tiled=True
-        ).astype(F32)
+        out_weight_grad = dot(middle_all, heads, 0, 0).astype(LOW)
         mixed_grads = attend_backward(plan, query, keys, values, heads, heads_grad, lse)
         flat_grad = jnp.concatenate(mixed_grads, axis=1)
         normed_terms = [dot(block_of(flat_grad, r), qkv_full, 1, 1) for r in range(size)]
         normed_grad = spread_blocks(lambda r: normed_terms[r], size)
         qkv_grad = dot(normed, flat_grad, 0, 0).astype(LOW)
-        qkv_sum = lax.psum_scatter(qkv_grad, "dp", scatter_dimension=0, tiled=True)
-        qkv_sum = qkv_sum.astype(F32).reshape(part, 3, local_width)
+        attention_sum = lax.psum_scatter(
+            jnp.concatenate([qkv_grad, out_weight_grad], axis=1),
+            "dp", scatter_dimension=0, tiled=True,
+        ).astype(F32)
+        qkv_sum = attention_sum[:, :width].reshape(part, 3, local_width)
+        out_weight_sum = attention_sum[:, width:].T
         query_sum = jnp.sum(mixed_grads[0], axis=0, dtype=F32).reshape(local_heads, HD)
         value_sum = jnp.sum(mixed_grads[2], axis=0, dtype=F32).reshape(local_heads, HD)
         qv_grad = jnp.concatenate([query_sum, value_sum], axis=1)

time: 535 us -> 521 us (0.974)
  blocking collectives: 71.1 us -> 42 us
  waiting for transfers between devices: 180 us -> 196 us
  local copies, waits for them, and re-layouts: 29.5 us -> 42.9 us
  matrix products: 108 us -> 97.6 us
    ppermute x24, waiting for transfers between devices: 101 us -> 149 us  [swap(): lax.ppermute(value, 'tensor', [(place, place ^ bit) for place in range(si...]
    unnamed x9 -> x6, waiting for transfers between devices: 54.6 us -> 22.7 us
    all_gather x1 -> x0, blocking collectives: 30.2 us -> none  [run(): out_full = lax.all_gather(out_weight, 'dp', axis=1, tiled=True)]
    all_gather x1, waiting for transfers between devices: 10.9 us -> 24.6 us  [run(): packed = lax.all_gather(packed, 'dp', axis=0)]
    reduce_scatter x2 -> x0, waiting for transfers between devices: 13.4 us -> none  [the longest x1 13.4 us: run(): qkv_sum = lax.psum_scatter(qkv_grad, 'dp', scatter_dimension=0, tiled=True)]
    unnamed x129 -> x142, local copies, waits for them, and re-layouts: 17.3 us -> 28.5 us
    dot_general x33, matrix products: 108 us -> 97.6 us  [dot(): lax.dot_general(left, right, (((left_dim,), (right_dim,)), ((), ())), pre...]
    concatenate x2 -> x5, other arithmetic: 1.11 us -> 7.85 us  [the longest x1 2.49 us: run(): jnp.concatenate([up_grad, down_grad], axis=1)]
  transfers between devices with their start and end apart: 31 -> 28, of which waited for: 9 -> 12; matrix products, arithmetic and copies ran while one was open for 26% -> 24% of each run, Pallas kernels for 13% -> 7%
where the time goes in v2:
time: 521 us; the launch traced here: 512 us
  waiting for transfers between devices  196 us (38%)
  matrix products  97.6 us (19%)
  Pallas kernels  69.7 us (13%)
  local copies, waits for them, and re-layouts  42.9 us (8%)
  blocking collectives  42 us (8%)
  other arithmetic  32.4 us (6%)
  between operations  15.9 us (3%)
  starting transfers between devices  15.2 us (3%)
    ppermute x24, waiting for transfers between devices, swap(): lax.ppermute(value, 'tensor', [(place, place ^ bit) for place in range(si...  149 us
    dot_general x33, matrix products, dot(): lax.dot_general(left, right, (((left_dim,), (right_dim,)), ((), ())), pre...  97.6 us
    unnamed x1, blocking collectives  36 us
    pallas_call x1, Pallas kernels, attend_forward(): pl.pallas_call(forward_kernel, grid=(count,), out_shape=(jax.ShapeDtypeSt...  35 us
    pallas_call x1, Pallas kernels, attend_backward(): pl.pallas_call(backward_kernel, grid=(count,), out_shape=(jax.ShapeDtypeS...  34.7 us
    unnamed x142, local copies, waits for them, and re-layouts  28.5 us
    all_gather x1, waiting for transfers between devices, run(): packed = lax.all_gather(packed, 'dp', axis=0)  24.6 us
    unnamed x6, waiting for transfers between devices  22.7 us
  transfers between devices with their start and end apart: 28, of which 12 were waited for; matrix products, arithmetic and copies ran while one was open for 24% of the time, Pallas kernels for 7%

profile of v2, /device:TPU:0, one launch (start us, length us, event | category | flops | bytes accessed | tf_op | source)
XLA Modules:
  0.0 511.5 jit_solution(13408126718426059011)
XLA Ops:
  22.7 18.4 %collective-permute-done.1 = bf16[512,1024]{1,0:T(8,128)(2,1)S(1)} collective-permute-done((bf16[512,1024]{1,0:T(8,128)(2,1)S(1)}, bf16[512,1024]{1,0:T(8,128)(2,1)S(1)}, u32[]{:S(2)}, u32[]{:S(2)}) %collective-permute-start.1) | collective-permute-done | bytes 1048608 | tf_op jit(solution)/shard_map/ppermute | solution.py:39
  45.1 24.6 %all-gather.6.cloned.1.call-done = bf16[1152,1024]{1,0:T(8,128)(2,1)} async-done(((bf16[144,1024]{1,0:T(8,128)(2,1)}), bf16[1152,1024]{1,0:T(8,128)(2,1)}) %all-gather.6.cloned.1.call-update) | async-done | bytes 2359312 | tf_op jit(solution)/shard_map/all_gather | solution.py:302
  69.6 3.1 slice.210
  77.5 7.2 %add_convert_fusion = bf16[2048,768]{1,0:T(8,128)(2,1)S(1)} fusion(f32[768]{0:T(1024)S(1)} %pad_maximum_fusion.8, bf16[1024,1024]{1,0:T(8,128)(2,1)S(1)} %bitcast.115, bf16[512,1024]{1,0:T(8,128)(2,1)S(1)} %get-tuple-element.153, bf16[512,1024]{1,0:T(8,128)(2,1)S(1)} %get-tuple-element.152, bf16[512,1024]{1,0:T(8,128)(2,1)S(1)} %get-tuple-element.151, ...), kind=kOutput, calls=%fused_computation.1 | convolution fusion | flops 3241148416 | bytes 8916992 | tf_op jit(solution)/shard_map/dot_general | solution.py:33
  84.9 35.0 %attend_forward.1 = (bf16[2048,256]{1,0:T(8,128)(2,1)S(1)}, f32[8,4,256]{2,1,0:T(4,128)S(1)}) custom-call(s32[8]{0:T(128)S(1)} %get-tuple-element.124.first_ref, s32[8]{0:T(128)S(1)} %get-tuple-element.123.clear_ref, s32[8]{0:T(128)S(1)} %get-tuple-element.169.phys_ref, f32[4]{0:T(128)S(1)} %power_multiply_fusion.slope_ref, ...), custom_call_target="tpu_custom_call" | custom-call | flops 2147483648 | bytes 4194304 | tf_op jit(solution)/shard_map/attend_forward/pallas_call | solution.py:221
  125.4 21.3 %collective-permute-done.7 = bf16[512,1024]{1,0:T(8,128)(2,1)} collective-permute-done((bf16[512,1024]{1,0:T(8,128)(2,1)S(1)}, bf16[512,1024]{1,0:T(8,128)(2,1)}, u32[]{:S(2)}, u32[]{:S(2)}) %collective-permute-start.7) | collective-permute-done | bytes 1048608 | tf_op jit(solution)/shard_map/ppermute | solution.py:39
  147.2 21.3 %collective-permute-done.5 = bf16[512,1024]{1,0:T(8,128)(2,1)S(1)} collective-permute-done((bf16[512,1024]{1,0:T(8,128)(2,1)S(1)}, bf16[512,1024]{1,0:T(8,128)(2,1)S(1)}, u32[]{:S(2)}, u32[]{:S(2)}) %collective-permute-start.5) | collective-permute-done | bytes 1048608 | tf_op jit(solution)/shard_map/ppermute | solution.py:39
  170.5 4.6 convolution_bitcast_fusion.1
  177.7 3.8 convolution_bitcast_fusion
  181.5 4.0 convolution_bitcast_fusion.2
  189.5 23.2 %collective-permute-done.10 = bf16[512,1024]{1,0:T(8,128)(2,1)} collective-permute-done((bf16[512,1024]{1,0:T(8,128)(2,1)}, bf16[512,1024]{1,0:T(8,128)(2,1)}, u32[]{:S(2)}, u32[]{:S(2)}) %collective-permute-start.10) | collective-permute-done | bytes 1048608 | tf_op jit(solution)/shard_map/ppermute | solution.py:39
  212.7 3.2 fusion.132
  218.5 4.0 fusion.130
  222.5 10.3 %fusion.77 = (bf16[512,1024]{0,1:T(8,128)(2,1)S(1)}, bf16[512,1024]{0,1:T(8,128)(2,1)}, bf16[512,1024]{0,1:T(8,128)(2,1)}, bf16[512,1024]{0,1:T(8,128)(2,1)S(1)}...) fusion(f32[512,1024]{0,1:T(8,128)S(1)} %copy-done.57, ...), kind=kOutput, calls=%fused_computation.102 | convolution fusion | flops 1121976320 | bytes 26218496 | tf_op jit(solution)/shard_map/dot_general | solution.py:33
  240.7 22.6 %collective-permute-done.14 = bf16[512,1024]{1,0:T(8,128)(2,1)S(1)} collective-permute-done((bf16[512,1024]{1,0:T(8,128)(2,1)S(1)}, bf16[512,1024]{1,0:T(8,128)(2,1)S(1)}, u32[]{:S(2)}, u32[]{:S(2)}) %collective-permute-start.14) | collective-permute-done | bytes 1048608 | tf_op jit(solution)/shard_map/ppermute | solution.py:39
  268.1 23.1 %collective-permute-done.15 = bf16[512,1024]{1,0:T(8,128)(2,1)S(1)} collective-permute-done((bf16[512,1024]{1,0:T(8,128)(2,1)S(1)}, bf16[512,1024]{1,0:T(8,128)(2,1)S(1)}, u32[]{:S(2)}, u32[]{:S(2)}) %collective-permute-start.15) | collective-permute-done | bytes 1048608 | tf_op jit(solution)/shard_map/ppermute | solution.py:39
  295.7 34.7 %attend_backward.1 = (bf16[2048,256]{1,0:T(8,128)(2,1)S(1)}, bf16[2048,256]{1,0:T(8,128)(2,1)S(1)}, bf16[2048,256]{1,0:T(8,128)(2,1)S(1)}) custom-call(s32[8]{0:T(128)S(1)} %get-tuple-element.124.first_ref, s32[8]{0:T(128)S(1)} %get-tuple-element.123.clear_ref, s32[8]{0:T(128)S(1)} %get-tuple-element.169.phys_ref, f32[4]{0:T(128)S(1)} %power_multiply_fusion.slope_ref, ...), custom_call_target="tpu_custom_call" | custom-call | flops 5368709120 | bytes 8388608 | tf_op jit(solution)/shard_map/attend_backward/pallas_call | solution.py:245
  332.7 3.7 convolution_convert_fusion
  339.6 4.0 copy.73
  343.6 8.0 %fusion.98 = bf16[1024,1024]{0,1:T(8,128)(2,1)S(1)} fusion(bf16[512,1024]{1,0:T(8,128)(2,1)} %collective-permute-done.8, bf16[512,1024]{1,0:T(8,128)(2,1)} %collective-permute-done.7, bf16[512,1024]{1,0:T(8,128)(2,1)} %collective-permute-done.6, bf16[512,1024]{1,0:T(8,128)(2,1)} %param.25, bf16[512,1024]{0,1:T(8,128)(2,1)} %get-tuple-element.43, ...), kind=kOutput, calls=%fused_computation.142 | convolution fusion | flops 4329570304 | bytes 10485760 | tf_op jit(solution)/shard_map/dot_general | solution.py:33
  356.3 6.4 %fusion.95 = bf16[1024,1024]{0,1:T(8,128)(2,1)S(1)} fusion(bf16[2048,1024]{0,1:T(8,128)(2,1)S(1)} %constant_dynamic-update-slice_fusion.9, bf16[512,1024]{1,0:T(8,128)(2,1)S(1)} %copy-done.52, bf16[512,1024]{1,0:T(8,128)(2,1)} %collective-permute-done.10, bf16[512,1024]{1,0:T(8,128)(2,1)} %collective-permute-done.9, bf16[512,1024]{1,0:T(8,128)(2,1)} %add_convert_fusion.5), kind=kOutput, calls=%fused_computation.141 | convolution fusion | flops 4312793088 | bytes 10485760 | tf_op jit(solution)/shard_map/dot_general | solution.py:33
  365.2 6.7 %copy.75 = bf16[1024,2048]{1,0:T(8,128)(2,1)} copy(bf16[1024,2048]{0,1:T(8,128)(2,1)} %pad_maximum_fusion.1) | data formatting | bytes 8388608
  376.9 4.1 fusion.172
  389.0 3.7 fusion.171
  394.8 4.4 convolution_convert_fusion.2
  399.5 3.6 add_convert_fusion.3
  403.4 15.6 %collective-permute-done.23 = bf16[512,1024]{1,0:T(8,128)(2,1)} collective-permute-done((bf16[512,1024]{1,0:T(8,128)(2,1)}, bf16[512,1024]{1,0:T(8,128)(2,1)}, u32[]{:S(2)}, u32[]{:S(2)}) %collective-permute-start.23) | collective-permute-done | bytes 1048608 | tf_op jit(solution)/shard_map/ppermute | solution.py:39
  419.0 3.5 fusion.51
  426.9 36.0 %all-reduce.2 = f32[64,128]{1,0:T(8,128)S(1)} all-reduce(f32[64,128]{1,0:T(8,128)S(1)} %reshape.393), channel_id=3, replica_groups=mesh['dp'=8,'tensor'=4] {'dp'}, use_global_device_ids=true, to_apply=%region_31.32.clone | all-reduce | flops 8192 | bytes 65536
  464.2 6.0 %psum.7 = f32[6,128]{1,0:T(8,128)S(1)} all-reduce(f32[6,128]{1,0:T(8,128)S(1)} %bitcast.140), channel_id=1, replica_groups=mesh['dp'=8,'tensor'=4] {'tensor'}, use_global_device_ids=true, to_apply=%region_32.33 | all-reduce | flops 768 | bytes 6144 | tf_op jit(solution)/shard_map/psum | solution.py:429
  471.3 4.7 add_convert_fusion.2
  478.7 22.6 %reduce-scatter.9.cloned.1.call-done = bf16[128,2048]{1,0:T(8,128)(2,1)} async-done(((bf16[1024,2048]{1,0:T(8,128)(2,1)}), bf16[128,2048]{1,0:T(8,128)(2,1)}) %reduce-scatter.9.cloned.1.call-update) | async-done | bytes 524304
  (314 shorter events, 98.2 us)
Async XLA Ops:
  7.2 62.5 %all-gather.6.cloned.1.call-start = ((), (), s32[]{:S(2)}) async-start(), calls=%async_computation.3 | async-start | bytes 2654208 | tf_op jit(solution)/shard_map/all_gather | solution.py:302
  14.8 155.7 %all-gather.4.cloned.1.call-start = ((), (), s32[]{:S(2)}) async-start(), calls=%async_computation.2 | async-start | bytes 4718592 | tf_op jit(solution)/shard_map/all_gather | solution.py:318
  14.8 26.2 %collective-permute-start.1 = (bf16[512,1024]{1,0:T(8,128)(2,1)S(1)}, bf16[512,1024]{1,0:T(8,128)(2,1)S(1)}, u32[]{:S(2)}, u32[]{:S(2)}) collective-permute-start(bf16[512,1024]{1,0:T(8,128)(2,1)S(1)} %copy-done.9), channel_id=1, source_target_pairs={{0,2},{1,3},{2,0},{3,1},{4,6},{5,7},{6,4},{7,5},{8,10},{9,11},{10,... | collective-permute-start | bytes 3145736 | tf_op jit(solution)/shard_map/ppermute | solution.py:39
  17.9 23.4 %collective-permute-start = (bf16[512,1024]{1,0:T(8,128)(2,1)S(1)}, bf16[512,1024]{1,0:T(8,128)(2,1)S(1)}, u32[]{:S(2)}, u32[]{:S(2)}) collective-permute-start(bf16[512,1024]{1,0:T(8,128)(2,1)S(1)} %copy-done.9), channel_id=1, source_target_pairs={{0,1},{1,0},{2,3},{3,2},{4,5},{5,4},{6,7},{7,6},{8,9},{9,8},{10,11... | collective-permute-start | bytes 3145736 | tf_op jit(solution)/shard_map/ppermute | solution.py:39
  20.8 455.2 %reduce-scatter.7.cloned.1.call-start = ((), (), s32[]{:S(2)}) async-start(), calls=%async_computation.4 | async-start | bytes 2359296
  41.0 2.7 collective-permute-start.2
  84.9 35.6 %copy-start.31 = (bf16[512,1024]{1,0:T(8,128)(2,1)S(1)}, bf16[512,1024]{1,0:T(8,128)(2,1)}, u32[]{:S(2)}) copy-start(bf16[512,1024]{1,0:T(8,128)(2,1)} %param.25) | copy-start | bytes 3145732
  120.5 2.7 collective-permute-start.4
  120.5 26.1 %collective-permute-start.7 = (bf16[512,1024]{1,0:T(8,128)(2,1)S(1)}, bf16[512,1024]{1,0:T(8,128)(2,1)}, u32[]{:S(2)}, u32[]{:S(2)}) collective-permute-start(bf16[512,1024]{1,0:T(8,128)(2,1)S(1)} %copy-done.31), channel_id=1, source_target_pairs={{0,2},{1,3},{2,0},{3,1},{4,6},{5,7},{6,4},{7,5},{8,10},{9,11},{10,... | collective-permute-start | bytes 3145736 | tf_op jit(solution)/shard_map/ppermute | solution.py:39
  122.7 24.5 %collective-permute-start.3 = (bf16[512,1024]{1,0:T(8,128)(2,1)S(1)}, bf16[512,1024]{1,0:T(8,128)(2,1)S(1)}, u32[]{:S(2)}, u32[]{:S(2)}) collective-permute-start(bf16[512,1024]{1,0:T(8,128)(2,1)S(1)} %convolution_convert_fusion.6), channel_id=1, source_target_pairs={{0,1},{1,0},{2,3},{3,2},{4,5},{5,4},{6,7},{7,6},{8,9},{9,8},{10,11... | collective-permute-start | bytes 3145736 | tf_op jit(solution)/shard_map/ppermute | solution.py:39
  123.7 44.9 %collective-permute-start.5 = (bf16[512,1024]{1,0:T(8,128)(2,1)S(1)}, bf16[512,1024]{1,0:T(8,128)(2,1)S(1)}, u32[]{:S(2)}, u32[]{:S(2)}) collective-permute-start(bf16[512,1024]{1,0:T(8,128)(2,1)S(1)} %add_convert_fusion.6), channel_id=1, source_target_pairs={{0,2},{1,3},{2,0},{3,1},{4,6},{5,7},{6,4},{7,5},{8,10},{9,11},{10,... | collective-permute-start | bytes 3145736 | tf_op jit(solution)/shard_map/ppermute | solution.py:39
  125.4 56.1 %collective-permute-start.6 = (bf16[512,1024]{1,0:T(8,128)(2,1)S(1)}, bf16[512,1024]{1,0:T(8,128)(2,1)}, u32[]{:S(2)}, u32[]{:S(2)}) collective-permute-start(bf16[512,1024]{1,0:T(8,128)(2,1)S(1)} %copy-done.31), channel_id=1, source_target_pairs={{0,1},{1,0},{2,3},{3,2},{4,5},{5,4},{6,7},{7,6},{8,9},{9,8},{10,11... | collective-permute-start | bytes 3145736 | tf_op jit(solution)/shard_map/ppermute | solution.py:39
  146.7 31.0 %collective-permute-start.8 = (bf16[512,1024]{1,0:T(8,128)(2,1)}, bf16[512,1024]{1,0:T(8,128)(2,1)}, u32[]{:S(2)}, u32[]{:S(2)}) collective-permute-start(bf16[512,1024]{1,0:T(8,128)(2,1)} %collective-permute-done.7), channel_id=1, source_target_pairs={{0,1},{1,0},{2,3},{3,2},{4,5},{5,4},{6,7},{7,6},{8,9},{9,8},{10,11... | collective-permute-start | bytes 3145736 | tf_op jit(solution)/shard_map/ppermute | solution.py:39
  185.9 78.5 %copy-start.7 = (f32[512,1024]{1,0:T(8,128)}, f32[512,1024]{1,0:T(8,128)S(1)}, u32[]{:S(2)}) copy-start(f32[512,1024]{1,0:T(8,128)S(1)} %get-tuple-element.122) | copy-start | bytes 6291460
  187.7 25.0 %collective-permute-start.10 = (bf16[512,1024]{1,0:T(8,128)(2,1)}, bf16[512,1024]{1,0:T(8,128)(2,1)}, u32[]{:S(2)}, u32[]{:S(2)}) collective-permute-start(bf16[512,1024]{1,0:T(8,128)(2,1)} %add_convert_fusion.5), channel_id=1, source_target_pairs={{0,2},{1,3},{2,0},{3,1},{4,6},{5,7},{6,4},{7,5},{8,10},{9,11},{10,... | collective-permute-start | bytes 3145736 | tf_op jit(solution)/shard_map/ppermute | solution.py:39
  189.3 29.2 %collective-permute-start.9 = (bf16[512,1024]{1,0:T(8,128)(2,1)}, bf16[512,1024]{1,0:T(8,128)(2,1)}, u32[]{:S(2)}, u32[]{:S(2)}) collective-permute-start(bf16[512,1024]{1,0:T(8,128)(2,1)} %add_convert_fusion.5), channel_id=1, source_target_pairs={{0,1},{1,0},{2,3},{3,2},{4,5},{5,4},{6,7},{7,6},{8,9},{9,8},{10,11... | collective-permute-start | bytes 3145736 | tf_op jit(solution)/shard_map/ppermute | solution.py:39
  212.7 9.8 %collective-permute-start.11 = (bf16[512,1024]{1,0:T(8,128)(2,1)}, bf16[512,1024]{1,0:T(8,128)(2,1)S(1)}, u32[]{:S(2)}, u32[]{:S(2)}) collective-permute-start(bf16[512,1024]{1,0:T(8,128)(2,1)} %collective-permute-done.10), channel_id=1, source_target_pairs={{0,1},{1,0},{2,3},{3,2},{4,5},{5,4},{6,7},{7,6},{8,9},{9,8},{10,11... | collective-permute-start | bytes 3145736 | tf_op jit(solution)/shard_map/ppermute | solution.py:39
  234.1 3.2 collective-permute-start.13
  235.9 4.7 collective-permute-start.12
  237.7 25.6 %collective-permute-start.14 = (bf16[512,1024]{1,0:T(8,128)(2,1)S(1)}, bf16[512,1024]{1,0:T(8,128)(2,1)S(1)}, u32[]{:S(2)}, u32[]{:S(2)}) collective-permute-start(bf16[512,1024]{1,0:T(8,128)(2,1)S(1)} %add_convert_fusion.4), channel_id=1, source_target_pairs={{0,2},{1,3},{2,0},{3,1},{4,6},{5,7},{6,4},{7,5},{8,10},{9,11},{10,... | collective-permute-start | bytes 3145736 | tf_op jit(solution)/shard_map/ppermute | solution.py:39
  266.5 24.8 %collective-permute-start.15 = (bf16[512,1024]{1,0:T(8,128)(2,1)S(1)}, bf16[512,1024]{1,0:T(8,128)(2,1)S(1)}, u32[]{:S(2)}, u32[]{:S(2)}) collective-permute-start(bf16[512,1024]{1,0:T(8,128)(2,1)S(1)} %get-tuple-element.115), channel_id=1, source_target_pairs={{0,2},{1,3},{2,0},{3,1},{4,6},{5,7},{6,4},{7,5},{8,10},{9,11},{10,... | collective-permute-start | bytes 3145736 | tf_op jit(solution)/shard_map/ppermute | solution.py:39
  268.1 24.1 %collective-permute-start.20 = (bf16[512,1024]{1,0:T(8,128)(2,1)S(1)}, bf16[512,1024]{1,0:T(8,128)(2,1)S(1)}, u32[]{:S(2)}, u32[]{:S(2)}) collective-permute-start(bf16[512,1024]{1,0:T(8,128)(2,1)S(1)} %get-tuple-element.115), channel_id=1, source_target_pairs={{0,1},{1,0},{2,3},{3,2},{4,5},{5,4},{6,7},{7,6},{8,9},{9,8},{10,11... | collective-permute-start | bytes 3145736 | tf_op jit(solution)/shard_map/ppermute | solution.py:39
  291.3 2.7 collective-permute-start.16
  343.6 157.8 %reduce-scatter.9.cloned.1.call-start = ((), (), s32[]{:S(2)}) async-start(), calls=%async_computation.5 | async-start | bytes 4718592
  381.0 8.0 %collective-permute-start.22 = (bf16[512,1024]{1,0:T(8,128)(2,1)}, bf16[512,1024]{1,0:T(8,128)(2,1)}, u32[]{:S(2)}, u32[]{:S(2)}) collective-permute-start(bf16[512,1024]{1,0:T(8,128)(2,1)} %get-tuple-element.138), channel_id=1, source_target_pairs={{0,1},{1,0},{2,3},{3,2},{4,5},{5,4},{6,7},{7,6},{8,9},{9,8},{10,11... | collective-permute-start | bytes 3145736 | tf_op jit(solution)/shard_map/ppermute | solution.py:39
  383.4 16.1 %collective-permute-start.18 = (bf16[512,1024]{1,0:T(8,128)(2,1)}, bf16[512,1024]{1,0:T(8,128)(2,1)}, u32[]{:S(2)}, u32[]{:S(2)}) collective-permute-start(bf16[512,1024]{1,0:T(8,128)(2,1)} %convolution_convert_fusion.1), channel_id=1, source_target_pairs={{0,1},{1,0},{2,3},{3,2},{4,5},{5,4},{6,7},{7,6},{8,9},{9,8},{10,11... | collective-permute-start | bytes 3145736 | tf_op jit(solution)/shard_map/ppermute | solution.py:39
  388.8 14.6 %collective-permute-start.21 = (bf16[512,1024]{1,0:T(8,128)(2,1)}, bf16[512,1024]{1,0:T(8,128)(2,1)S(1)}, u32[]{:S(2)}, u32[]{:S(2)}) collective-permute-start(bf16[512,1024]{1,0:T(8,128)(2,1)} %get-tuple-element.136), channel_id=1, source_target_pairs={{0,1},{1,0},{2,3},{3,2},{4,5},{5,4},{6,7},{7,6},{8,9},{9,8},{10,11... | collective-permute-start | bytes 3145736 | tf_op jit(solution)/shard_map/ppermute | solution.py:39
  392.7 26.3 %collective-permute-start.23 = (bf16[512,1024]{1,0:T(8,128)(2,1)}, bf16[512,1024]{1,0:T(8,128)(2,1)}, u32[]{:S(2)}, u32[]{:S(2)}) collective-permute-start(bf16[512,1024]{1,0:T(8,128)(2,1)} %get-tuple-element.137), channel_id=1, source_target_pairs={{0,2},{1,3},{2,0},{3,1},{4,6},{5,7},{6,4},{7,5},{8,10},{9,11},{10,... | collective-permute-start | bytes 3145736 | tf_op jit(solution)/shard_map/ppermute | solution.py:39
  399.2 72.1 %collective-permute-start.17 = (bf16[512,1024]{1,0:T(8,128)(2,1)}, bf16[512,1024]{1,0:T(8,128)(2,1)}, u32[]{:S(2)}, u32[]{:S(2)}) collective-permute-start(bf16[512,1024]{1,0:T(8,128)(2,1)} %convolution_convert_fusion.2), channel_id=1, source_target_pairs={{0,1},{1,0},{2,3},{3,2},{4,5},{5,4},{6,7},{7,6},{8,9},{9,8},{10,11... | collective-permute-start | bytes 3145736 | tf_op jit(solution)/shard_map/ppermute | solution.py:39
  403.1 68.2 %collective-permute-start.19 = (bf16[512,1024]{1,0:T(8,128)(2,1)}, bf16[512,1024]{1,0:T(8,128)(2,1)}, u32[]{:S(2)}, u32[]{:S(2)}) collective-permute-start(bf16[512,1024]{1,0:T(8,128)(2,1)} %add_convert_fusion.3), channel_id=1, source_target_pairs={{0,2},{1,3},{2,0},{3,1},{4,6},{5,7},{6,4},{7,5},{8,10},{9,11},{10,... | collective-permute-start | bytes 3145736 | tf_op jit(solution)/shard_map/ppermute | solution.py:39
  425.0 46.3 %copy-start.8 = (f32[512,1024]{1,0:T(8,128)S(1)}, f32[512,1024]{1,0:T(8,128)}, u32[]{:S(2)}) copy-start(f32[512,1024]{1,0:T(8,128)} %copy-done.7) | copy-start | bytes 6291460
  425.0 46.3 %copy-start.58 = (bf16[512,1024]{0,1:T(8,128)(2,1)S(1)}, bf16[512,1024]{0,1:T(8,128)(2,1)}, u32[]{:S(2)}) copy-start(bf16[512,1024]{0,1:T(8,128)(2,1)} %get-tuple-element.40) | copy-start | bytes 3145732
  (57 other events, 478.7 us)
Sparse Core Ops, SparseCore 0:
  14.9 54.6 all-gather.5
  72.3 73.7 all-gather.3
  343.7 66.4 reduce-scatter.6
  413.7 87.5 reduce-scatter.8
